TPU v7x, 768 devices: a whole 4x8x12 slice. The times are simulated.
768 devices in a mesh: tile: 128 (over z_hi, y, x, core), scene: 6 (over z_lo).
Axes of the slice: x: 4, y: 8, z: 12 (z_hi: 2, z_lo: 6; z = z_hi * 6 + z_lo), core: 2. Of those that a mesh axis runs over, the one named last changes fastest.
Arguments:
- features: bfloat16 [6, 384, 64, 128], P('scene', 'tile'), may hold values from -6 to 6
- cotangent: bfloat16 [6, 384, 64, 128], P('scene', 'tile'), may hold values from -6 to 6
- blocks: int32 [6, 384], P('scene', 'tile'), may hold values from 0 to 8, as said below
- w_first: bfloat16 [27, 128, 128], replicated, may hold values from -0.109375 to 0.109375
- w_second: bfloat16 [27, 128, 128], replicated, may hold values from -0.109375 to 0.109375
Outputs:
- block_out: bfloat16 [6, 384, 64, 128], P('scene', 'tile')
- input_grad: bfloat16 [6, 384, 64, 128], P('scene', 'tile')
- grad_first: float32 [27, 16384], P(None, 'tile')
- grad_second: float32 [27, 16384], P(None, 'tile')
Inputs may be any that keep to these rules, and one draw needn't show every extreme that they name: In each tile's 3 slots the non-empty ones come first and name distinct blocks of 0 to 7; the rest hold 8. Every tile has at least 1 non-empty slot; in every scene some tile has all 3 slots non-empty and some other tile the fewest.
All inputs are finite; a program needn't handle non-finite values.
Results may differ from a plain program's by a relative error of at most 0.0029.
Values may be sent and summed in bfloat16 or wider, within the bound.
No kernel may reach another device: no remote copies, remote signals or barrier semaphores. Data moves between devices by JAX's collectives and lax.ppermute only.
A program may use at most 32 MiB of HBM per device.

v0:
```python
import jax
import jax.numpy as jnp
from jax import lax
from jax.sharding import PartitionSpec as P

BY = 2
BZ = 4


def padded_2(value, sides, width):
    for axis, dim in sides:
        size, length = (lax.axis_size(axis), value.shape[dim])
        up = [(i, (i + 1) % size) for i in range(size - 1)]
        down = [(j, i) for i, j in up]
        last = lax.slice_in_dim(value, length - width, length, axis=dim)
        leading = lax.slice_in_dim(value, 0, width, axis=dim)
        before = lax.ppermute(last, axis, up)
        after = lax.ppermute(leading, axis, down)
        value = jnp.concatenate([before, value, after], axis=dim)
    return value


def build_slab(rows, slot_blocks):
    channels = rows.shape[-1]
    holder = jnp.zeros((BY * BZ + 1, 64, channels), rows.dtype).at[slot_blocks].set(rows)[: BY * BZ]
    shaped = holder.reshape(BY, BZ, 4, 4, 4, channels).transpose(2, 0, 3, 1, 4, 5)
    return shaped.reshape(4, 4 * BY, 4 * BZ, channels)


def cut_windows(padded, slot_blocks):
    channels = padded.shape[-1]
    clipped = jnp.minimum(slot_blocks, BY * BZ - 1)

    def single(block_id):
        anchor = jnp.zeros((), jnp.int32)
        return lax.dynamic_slice(
            padded, (anchor, 4 * (block_id // BZ), 4 * (block_id % BZ), anchor), (6, 6, 6, channels)
        )

    return jax.vmap(single)(clipped)


def apply_taps(windows, weights, transposed):
    slot_count = windows.shape[0]
    channels = windows.shape[-1]
    summed = jnp.zeros((slot_count * 64, weights.shape[-1]), jnp.float32)
    for along_x in range(3):
        for along_y in range(3):
            for along_z in range(3):
                tap_index = along_x * 9 + along_y * 3 + along_z
                if transposed:
                    corner = (2 - along_x, 2 - along_y, 2 - along_z)
                    matrix = weights[tap_index].T
                else:
                    corner = (along_x, along_y, along_z)
                    matrix = weights[tap_index]
                window_piece = windows[
                    :,
                    corner[0] : corner[0] + 4,
                    corner[1] : corner[1] + 4,
                    corner[2] : corner[2] + 4,
                    :,
                ]
                summed = summed + jnp.dot(
                    window_piece.reshape(slot_count * 64, channels),
                    matrix,
                    preferred_element_type=jnp.float32,
                )
    return summed.reshape(slot_count, 64, -1)


def weight_terms(windows, gradient):
    channels = windows.shape[-1]
    gradient_rows = gradient.reshape(-1, gradient.shape[-1])
    tap_terms = []
    for along_x in range(3):
        for along_y in range(3):
            for along_z in range(3):
                window_piece = windows[
                    :, along_x : along_x + 4, along_y : along_y + 4, along_z : along_z + 4, :
                ]
                tap_terms.append(
                    lax.dot_general(
                        window_piece.reshape(-1, channels),
                        gradient_rows,
                        (((0,), (0,)), ((), ())),
                        preferred_element_type=jnp.float32,
                    )
                )
    return jnp.stack(tap_terms)


def silu_slope(values):
    sigmoid_value = jax.nn.sigmoid(values)
    return sigmoid_value * (1.0 + values * (1.0 - sigmoid_value))


def pad_sides(extended):
    return jnp.pad(extended, ((0, 0), (1, 1), (1, 1), (0, 0)))


def on_device(features, cotangent, blocks, w_first, w_second):
    slot_blocks = blocks[0]
    inputs = features[0]
    upstream = cotangent[0]
    channels = inputs.shape[-1]
    live_mask = (slot_blocks < BY * BZ).astype(jnp.float32)[:, None, None]
    input_slab = build_slab(inputs, slot_blocks)
    upstream_slab = build_slab(upstream, slot_blocks)
    stacked_rims = padded_2(jnp.stack([input_slab, upstream_slab]), (("tile", 1),), 1)
    input_pad = pad_sides(stacked_rims[0])
    upstream_pad = pad_sides(stacked_rims[1])
    input_windows = cut_windows(input_pad, slot_blocks)
    first_act = apply_taps(input_windows, w_first, False)
    hidden = jax.nn.silu(first_act).astype(jnp.bfloat16)
    hidden_pad = pad_sides(padded_2(build_slab(hidden, slot_blocks), (("tile", 0),), 1))
    hidden_windows = cut_windows(hidden_pad, slot_blocks)
    second_act = apply_taps(hidden_windows, w_second, False)
    output = (live_mask * (inputs.astype(jnp.float32) + second_act)).astype(jnp.bfloat16)
    hidden_grad = apply_taps(cut_windows(upstream_pad, slot_blocks), w_second, True)
    first_grad = (live_mask * hidden_grad * silu_slope(first_act)).astype(jnp.bfloat16)
    masked_upstream = (upstream.astype(jnp.float32) * live_mask).astype(jnp.bfloat16)
    second_terms = weight_terms(hidden_windows, masked_upstream).reshape(27, channels * channels)
    grad_pad = pad_sides(padded_2(build_slab(first_grad, slot_blocks), (("tile", 0),), 1))
    back_conv = apply_taps(cut_windows(grad_pad, slot_blocks), w_first, True)
    input_out = (live_mask * (upstream.astype(jnp.float32) + back_conv)).astype(jnp.bfloat16)
    first_terms = weight_terms(input_windows, first_grad).reshape(27, channels * channels)
    first_share, second_share = (
        lax.psum_scatter(first_terms, "tile", scatter_dimension=1, tiled=True),
        lax.psum_scatter(second_terms, "tile", scatter_dimension=1, tiled=True),
    )
    first_total, second_total = lax.psum((first_share, second_share), "scene")
    return (output[None], input_out[None], first_total, second_total)


def solution(mesh):
    return jax.shard_map(
        on_device,
        mesh=mesh,
        in_specs=(
            P("scene", "tile", None, None),
            P("scene", "tile", None, None),
            P("scene", "tile"),
            P(),
            P(),
        ),
        out_specs=(
            P("scene", "tile", None, None),
            P("scene", "tile", None, None),
            P(None, "tile"),
            P(None, "tile"),
        ),
        check_vma=False,
    )
```

profile of v0, /device:TPU:1, one launch (start us, length us, event | category | flops | bytes accessed | tf_op | source)
XLA Modules:
  0.0 2075.1 jit_solution(14145742479378415635)
XLA Ops:
  7.2 0.7 fusion.236
  7.9 1.4 scatter_fusion.1
  9.4 1.4 scatter_fusion
  10.8 0.2 fusion.4
  11.1 4.5 collective-permute-start
  15.6 9.2 collective-permute-start.1
  25.0 0.8 collective-permute-done.1
  25.8 0.4 pad_maximum_fusion
  26.4 0.6 gather_fusion.2
  27.1 0.4 fusion.239
  27.6 0.6 gather_fusion
  28.4 0.4 fusion.243
  42.4 0.8 fusion.255
  43.2 0.8 fusion.254
  44.0 0.8 fusion.253
  44.8 0.8 fusion.252
  45.6 0.8 fusion.251
  46.5 0.8 fusion.250
  47.3 0.8 fusion.249
  48.1 0.8 fusion.248
  48.9 0.8 fusion.247
  49.9 0.6 scatter_fusion.2
  50.6 0.6 scatter_fusion.3
  51.3 0.7 copy.41
  52.0 0.7 copy.44
  52.6 2.3 collective-permute-start.3
  54.9 3.3 collective-permute-start.2
  58.4 0.7 copy.100
  59.1 0.7 copy.103
  59.7 1.9 collective-permute-start.5
  61.6 3.6 collective-permute-start.4
  65.3 6.9 stack.199
  72.3 0.2 reduce-scatter.5.cloned.1.call-start
  72.5 1.1 select_maximum_fusion.2
  73.6 0.6 gather_fusion.1
  74.2 1.1 fusion.241
  75.5 1.1 select_maximum_fusion
  76.6 0.6 gather_fusion.3
  77.4 0.4 fusion.237
  87.9 0.7 fusion.7
  88.8 0.2 fusion.299
  89.4 0.2 fusion.296
  90.0 0.2 fusion.293
  92.4 0.2 fusion.281
  93.9 5.4 stack.227
  99.4 973.7 %reduce-scatter.3.cloned.1.call-done = f32[27,128]{1,0:T(8,128)} async-done(((f32[27,16384]{1,0:T(8,128)}), f32[27,128]{1,0:T(8,128)}) %reduce-scatter.3.cloned.1.call-update) | async-done | bytes 13840 | tf_op jit(solution)/shard_map/reduce_scatter | solution.py:129
  1073.1 967.2 %reduce-scatter.5.cloned.1.call-done = f32[27,128]{1,0:T(8,128)} async-done(((f32[27,16384]{1,0:T(8,128)}), f32[27,128]{1,0:T(8,128)}) %reduce-scatter.5.cloned.1.call-update) | async-done | bytes 13840 | tf_op jit(solution)/shard_map/reduce_scatter | solution.py:130
  2040.3 28.0 %all-reduce.4 = (f32[27,128]{1,0:T(8,128)}, f32[27,128]{1,0:T(8,128)}) all-reduce(f32[27,128]{1,0:T(8,128)} %reduce-scatter.3.cloned.1.call-done, f32[27,128]{1,0:T(8,128)} %reduce-scatter.5.cloned.1.call-done), channel_id=1, replica_groups=mesh['tile'=128,'scene'=6] {'scene'}, use_global_device_ids=true, to_apply=%region_5.6 | all-reduce | flops 6912 | bytes 55296 | tf_op jit(solution)/shard_map/psum | solution.py:132
  (316 shorter events, 27.6 us)
Async XLA Ops:
  7.2 17.6 copy-start.10
  7.2 1065.9 %reduce-scatter.3.cloned.1.call-start = ((), (), s32[]{:S(2)}) async-start(), calls=%async_computation.2 | async-start | bytes 2113536 | tf_op jit(solution)/shard_map/reduce_scatter | solution.py:129
  11.1 13.9 collective-permute-start
  15.6 10.2 collective-permute-start.1
  29.1 1.2 copy-start.1
  29.8 1.8 copy-start
  52.6 19.9 collective-permute-start.3
  54.9 17.6 collective-permute-start.2
  59.7 15.7 collective-permute-start.5
  61.6 13.8 collective-permute-start.4
  72.3 1968.0 %reduce-scatter.5.cloned.1.call-start = ((), (), s32[]{:S(2)}) async-start(), calls=%async_computation.3 | async-start | bytes 2113536 | tf_op jit(solution)/shard_map/reduce_scatter | solution.py:130
  77.4 1.2 copy-start.9
  77.4 1.3 copy-start.8
  77.4 1.3 copy-start.7
  77.4 1.3 copy-start.6
  77.4 1.3 copy-start.5
  77.4 1.4 copy-start.4
  85.4 2.5 copy-start.2
  85.4 2.5 copy-start.3
Sparse Core Ops, SparseCore 0:
  72.4 1000.6 reduce-scatter.2
  1076.4 963.7 reduce-scatter.4
where the time goes:
time: 2090 us; the launch traced here: 2080 us
  waiting for transfers between devices  1940 us (93%)
  matrix products  32 us (2%)
  blocking collectives  28 us (1%)
  local copies, waits for them, and re-layouts  27.4 us (1%)
  starting transfers between devices  25.1 us (1%)
    reduce_scatter x1, waiting for transfers between devices, on_device(): lax.psum_scatter(first_terms, 'tile', scatter_dimension=1, tiled=True)  974 us
    reduce_scatter x1, waiting for transfers between devices, on_device(): lax.psum_scatter(second_terms, 'tile', scatter_dimension=1, tiled=True)  967 us
  transfers between devices with their start and end apart: 8, of which 3 were waited for; matrix products, arithmetic and copies ran while one was open for 2% of the time, Pallas kernels for 0%

commit v1 on v0

--- a/solution.py
+++ b/solution.py
@@ -1,10 +1,11 @@
 import jax
 import jax.numpy as jnp
 from jax import lax
-from jax.sharding import PartitionSpec as P
+from jax.sharding import Mesh, PartitionSpec as P
 
 BY = 2
 BZ = 4
+TILE = ("zh", "y", "x", "c")
 
 
 def padded_2(value, sides, width):
@@ -99,6 +100,25 @@
     return jnp.pad(extended, ((0, 0), (1, 1), (1, 1), (0, 0)))
 
 
+def folded(pieces):
+    return pieces.astype(jnp.float32).sum(axis=0)
+
+
+def summed_terms(first_terms, second_terms):
+    halves = jnp.stack([first_terms, second_terms])
+    parts = halves.reshape(54, 2, 8, 4, 2, 128).transpose(4, 3, 2, 1, 0, 5)
+    core = lax.axis_index("c")
+    kept = lax.dynamic_index_in_dim(parts, core, 0, keepdims=False)
+    sent = lax.dynamic_index_in_dim(parts, 1 - core, 0, keepdims=False)
+    got = lax.ppermute(sent.astype(jnp.bfloat16), "c", [(0, 1), (1, 0)])
+    chip = (kept + got.astype(jnp.float32)).astype(jnp.bfloat16)
+    along_x = folded(lax.all_to_all(chip, "x", 0, 0, tiled=True).reshape(4, 8, 2, 54, 128))
+    along_y = folded(lax.all_to_all(along_x, "y", 0, 0, tiled=True))
+    spread = jnp.broadcast_to(along_y[:, None], (2, 6, 54, 128)).reshape(12, 54, 128)
+    total = folded(lax.all_to_all(spread, ("zh", "scene"), 0, 0, tiled=True))
+    return total[:27], total[27:]
+
+
 def on_device(features, cotangent, blocks, w_first, w_second):
     slot_blocks = blocks[0]
     inputs = features[0]
@@ -107,13 +127,13 @@
     live_mask = (slot_blocks < BY * BZ).astype(jnp.float32)[:, None, None]
     input_slab = build_slab(inputs, slot_blocks)
     upstream_slab = build_slab(upstream, slot_blocks)
-    stacked_rims = padded_2(jnp.stack([input_slab, upstream_slab]), (("tile", 1),), 1)
+    stacked_rims = padded_2(jnp.stack([input_slab, upstream_slab]), ((TILE, 1),), 1)
     input_pad = pad_sides(stacked_rims[0])
     upstream_pad = pad_sides(stacked_rims[1])
     input_windows = cut_windows(input_pad, slot_blocks)
     first_act = apply_taps(input_windows, w_first, False)
     hidden = jax.nn.silu(first_act).astype(jnp.bfloat16)
-    hidden_pad = pad_sides(padded_2(build_slab(hidden, slot_blocks), (("tile", 0),), 1))
+    hidden_pad = pad_sides(padded_2(build_slab(hidden, slot_blocks), ((TILE, 0),), 1))
     hidden_windows = cut_windows(hidden_pad, slot_blocks)
     second_act = apply_taps(hidden_windows, w_second, False)
     output = (live_mask * (inputs.astype(jnp.float32) + second_act)).astype(jnp.bfloat16)
@@ -121,34 +141,31 @@
     first_grad = (live_mask * hidden_grad * silu_slope(first_act)).astype(jnp.bfloat16)
     masked_upstream = (upstream.astype(jnp.float32) * live_mask).astype(jnp.bfloat16)
     second_terms = weight_terms(hidden_windows, masked_upstream).reshape(27, channels * channels)
-    grad_pad = pad_sides(padded_2(build_slab(first_grad, slot_blocks), (("tile", 0),), 1))
+    grad_pad = pad_sides(padded_2(build_slab(first_grad, slot_blocks), ((TILE, 0),), 1))
     back_conv = apply_taps(cut_windows(grad_pad, slot_blocks), w_first, True)
     input_out = (live_mask * (upstream.astype(jnp.float32) + back_conv)).astype(jnp.bfloat16)
     first_terms = weight_terms(input_windows, first_grad).reshape(27, channels * channels)
-    first_share, second_share = (
-        lax.psum_scatter(first_terms, "tile", scatter_dimension=1, tiled=True),
-        lax.psum_scatter(second_terms, "tile", scatter_dimension=1, tiled=True),
-    )
-    first_total, second_total = lax.psum((first_share, second_share), "scene")
+    first_total, second_total = summed_terms(first_terms, second_terms)
     return (output[None], input_out[None], first_total, second_total)
 
 
 def solution(mesh):
+    split = Mesh(mesh.devices.reshape(2, 8, 4, 2, 6), TILE + ("scene",))
     return jax.shard_map(
         on_device,
-        mesh=mesh,
+        mesh=split,
         in_specs=(
-            P("scene", "tile", None, None),
-            P("scene", "tile", None, None),
-            P("scene", "tile"),
+            P("scene", TILE, None, None),
+            P("scene", TILE, None, None),
+            P("scene", TILE),
             P(),
             P(),
         ),
         out_specs=(
-            P("scene", "tile", None, None),
-            P("scene", "tile", None, None),
-            P(None, "tile"),
-            P(None, "tile"),
+            P("scene", TILE, None, None),
+            P("scene", TILE, None, None),
+            P(None, TILE),
+            P(None, TILE),
         ),
         check_vma=False,
     )

time: 2090 us -> 221 us (0.11)
  the two profiles are of different devices: /device:TPU:1 before, /device:TPU:2 now
where the time goes in v1:
time: 221 us; the launch traced here: 220 us
  blocking collectives  89.1 us (40%)
  matrix products  43.9 us (20%)
  local copies, waits for them, and re-layouts  43.7 us (20%)
  starting transfers between devices  16.3 us (7%)
  other arithmetic  11.8 us (5%)
  waiting for transfers between devices  11.5 us (5%)
  between operations  3.49 us (2%)
    all_to_all x1, blocking collectives, summed_terms(): along_y = folded(lax.all_to_all(along_x, 'y', 0, 0, tiled=True))  44.5 us
    dot_general x54, matrix products, weight_terms(): lax.dot_general(window_piece.reshape(-1, channels), gradient_rows, (((0,)...  28 us
    all_to_all x1, blocking collectives, summed_terms(): total = folded(lax.all_to_all(spread, ('zh', 'scene'), 0, 0, tiled=True))  27.8 us
    all_to_all x1, blocking collectives, summed_terms(): lax.all_to_all(chip, 'x', 0, 0, tiled=True).reshape(4, 8, 2, 54, 128)  16.7 us
    dot_general x108, matrix products, apply_taps(): jnp.dot(window_piece.reshape(slot_count * 64, channels), matrix, preferre...  15.9 us
    another operation x2, local copies, waits for them, and re-layouts, weight_terms(): return jnp.stack(tap_terms)  13 us
    ppermute x3, waiting for transfers between devices, padded_2(): before = lax.ppermute(last, axis, up)  11 us
    ppermute x3, starting transfers between devices, padded_2(): after = lax.ppermute(leading, axis, down)  6.98 us
  transfers between devices with their start and end apart: 7, of which 2 were waited for; matrix products, arithmetic and copies ran while one was open for 8% of the time, Pallas kernels for 0%

profile of v1, /device:TPU:2, one launch (start us, length us, event | category | flops | bytes accessed | tf_op | source)
XLA Modules:
  0.0 219.7 jit_solution(6984242981472735695)
XLA Ops:
  1.4 1.4 scatter_fusion
  2.9 1.4 scatter_fusion.1
  4.5 1.9 collective-permute-start.1
  6.5 2.4 %collective-permute-start = (bf16[2,1,8,16,128]{4,1,3,2,0:T(2,128)(2,1)S(1)}, bf16[2,1,8,16,128]{4,1,3,2,0:T(2,128)(2,1)S(1)}, u32[]{:S(2)}, u32[]{:S(2)}) collective-permute-start(bf16[2,1,8,16,128]{4,1,3,2,0:T(2,128)(2,1)S(1)} %get-tuple-element.6), channel_id=1, source_target_pairs={{0,6},{6,12},{12,18},{18,24},{24,30},{30,36},{36,42},{42,48},{48,5... | collective-permute-start | bytes 196616 | tf_op jit(solution)/shard_map/ppermute | solution.py:18
  9.6 11.0 %collective-permute-done = bf16[2,1,8,16,128]{4,1,3,2,0:T(2,128)(2,1)S(1)} collective-permute-done((bf16[2,1,8,16,128]{4,1,3,2,0:T(2,128)(2,1)S(1)}, bf16[2,1,8,16,128]{4,1,3,2,0:T(2,128)(2,1)S(1)}, u32[]{:S(2)}, u32[]{:S(2)}) %collective-permute-start) | collective-permute-done | bytes 65568 | tf_op jit(solution)/shard_map/ppermute | solution.py:18
  22.0 1.0 fusion.239
  35.2 0.8 fusion.252
  36.0 0.8 fusion.253
  36.9 0.8 fusion.254
  37.7 0.8 fusion.255
  38.5 0.8 fusion.256
  40.1 0.8 fusion.258
  41.0 0.8 fusion.259
  41.8 0.8 fusion.260
  44.2 0.8 fusion.263
  45.8 0.8 fusion.265
  47.5 0.8 fusion.267
  48.3 0.8 fusion.268
  49.1 0.8 fusion.269
  50.8 0.8 fusion.271
  51.6 0.8 fusion.272
  53.2 0.8 fusion.274
  55.5 1.9 collective-permute-start.5
  58.2 2.4 %collective-permute-start.4 = (bf16[1,8,16,128]{3,0,2,1:T(2,128)(2,1)}, bf16[1,8,16,128]{3,0,2,1:T(2,128)(2,1)}, u32[]{:S(2)}, u32[]{:S(2)}) collective-permute-start(bf16[1,8,16,128]{3,0,2,1:T(2,128)(2,1)} %copy.474), channel_id=1, source_target_pairs={{0,6},{6,12},{12,18},{18,24},{24,30},{30,36},{36,42},{42,48},{48,5... | collective-permute-start | bytes 98312 | tf_op jit(solution)/shard_map/ppermute | solution.py:18
  62.1 3.1 %collective-permute-start.3 = (bf16[1,8,16,128]{3,0,2,1:T(2,128)(2,1)}, bf16[1,8,16,128]{3,0,2,1:T(2,128)(2,1)}, u32[]{:S(2)}, u32[]{:S(2)}) collective-permute-start(bf16[1,8,16,128]{3,0,2,1:T(2,128)(2,1)} %copy.418), channel_id=1, source_target_pairs={{6,0},{12,6},{18,12},{24,18},{30,24},{36,30},{42,36},{48,42},{54,4... | collective-permute-start | bytes 98312 | tf_op jit(solution)/shard_map/ppermute | solution.py:19
  66.0 2.1 collective-permute-start.2
  68.1 6.0 %stack.202 = f32[1,27,16384]{2,1,0:T(8,128)S(1)} concatenate(f32[1,1,16384]{2,1,0:T(1,128)S(1)} %bitcast.854, f32[1,1,16384]{2,1,0:T(1,128)S(1)} %bitcast.855, f32[1,1,16384]{2,1,0:T(1,128)S(1)} %bitcast.856, f32[1,1,16384]{2,1,0:T(1,128)S(1)} %bitcast.857, f32[1,1,16384]{2,1,0:T(1,128)} %bitcast.858, f32[1,1,16384]{2,1,0:T(1,128)} %bitcast.859, f32[1,1,16384]{2,1,0:T(1,128)} %bitcast.860, ...), dimensions={1} | concatenate | bytes 3538944 | tf_op jit(solution)/shard_map/stack | solution.py:91
  74.1 1.9 select_maximum_fusion
  76.0 1.6 gather_fusion.3
  77.6 1.1 fusion.237
  79.5 1.9 select_maximum_fusion.2
  81.4 1.6 gather_fusion.1
  99.4 0.8 fusion.297
  100.2 0.8 fusion.298
  101.1 0.8 fusion.299
  101.9 0.8 fusion.300
  102.7 0.8 fusion.301
  103.5 6.9 %stack.230 = f32[1,27,16384]{2,1,0:T(8,128)} concatenate(f32[1,1,16384]{2,1,0:T(1,128)S(1)} %bitcast.881, f32[1,1,16384]{2,1,0:T(1,128)S(1)} %bitcast.882, f32[1,1,16384]{2,1,0:T(1,128)S(1)} %bitcast.883, f32[1,1,16384]{2,1,0:T(1,128)S(1)} %bitcast.884, f32[1,1,16384]{2,1,0:T(1,128)S(1)} %bitcast.885, f32[1,1,16384]{2,1,0:T(1,128)S(1)} %bitcast.886, ...), dimensions={1} | concatenate | bytes 3538944 | tf_op jit(solution)/shard_map/stack | solution.py:91
  110.5 3.8 %pad_maximum_fusion = f32[2,27,16384]{2,1,0:T(8,128)} fusion(f32[1,27,16384]{2,1,0:T(8,128)} %stack.230, f32[1,27,16384]{2,1,0:T(8,128)S(1)} %stack.202), kind=kLoop, calls=%fused_computation.8 | loop fusion | flops 884736 | bytes 7077888 | tf_op jit(solution)/shard_map/stack | solution.py:108
  114.3 4.8 %reshape.963 = f32[54,2,8,4,2,128]{5,4,3,2,1,0:T(2,128)S(1)} reshape(f32[2,27,16384]{2,1,0:T(8,128)} %pad_maximum_fusion) | data formatting | bytes 7077888 | tf_op jit(solution)/shard_map/reshape | solution.py:109
  119.2 1.9 convert_bitcast_fusion
  121.2 1.6 copy.506
  122.8 2.4 %collective-permute-start.6 = (bf16[4,8,2,54,128]{4,0,1,2,3:T(4,128)(2,1)}, bf16[4,8,2,54,128]{4,0,1,2,3:T(4,128)(2,1)}, u32[]{:S(2)}, u32[]{:S(2)}) collective-permute-start(bf16[4,8,2,54,128]{4,0,1,2,3:T(4,128)(2,1)} %copy.506), channel_id=1, source_target_pairs={{0,6},{6,0},{1,7},{7,1},{2,8},{8,2},{3,9},{9,3},{4,10},{10,4},{5,1... | collective-permute-start | bytes 2654216 | tf_op jit(solution)/shard_map/ppermute | solution.py:113
  125.2 1.9 constant_dynamic-slice_fusion
  127.6 1.7 add_convert_fusion
  129.5 16.7 %all_to_all.15 = bf16[4,8,2,54,128]{4,1,2,3,0:T(8,128)(2,1)S(1)} all-to-all(bf16[4,8,2,54,128]{4,1,2,3,0:T(8,128)(2,1)S(1)} %copy.507), channel_id=1, replica_groups=mesh['zh'=2,'y'=8,'x'=4,'c'=2,'scene'=6] {'x'}, dimensions={0} | all-to-all | bytes 1769472 | tf_op jit(solution)/shard_map/all_to_all | solution.py:115
  146.6 44.5 %all_to_all.16 = f32[8,2,54,128]{3,1,2,0:T(2,128)S(1)} all-to-all(f32[8,2,54,128]{3,1,2,0:T(2,128)S(1)} %copy.509), channel_id=1, replica_groups=mesh['zh'=2,'y'=8,'x'=4,'c'=2,'scene'=6] {'y'}, dimensions={0} | all-to-all | bytes 884736 | tf_op jit(solution)/shard_map/all_to_all | solution.py:116
  191.3 27.8 %all_to_all.17 = f32[12,54,128]{2,1,0:T(8,128)S(1)} all-to-all(f32[12,54,128]{2,1,0:T(8,128)S(1)} %bitcast.732), channel_id=1, replica_groups=mesh['zh'=2,'y'=8,'x'=4,'c'=2,'scene'=6] {'zh','scene'}, dimensions={0} | all-to-all | bytes 663552 | tf_op jit(solution)/shard_map/all_to_all | solution.py:118
  (385 shorter events, 42.1 us)
Async XLA Ops:
  0.6 8.2 %copy-start.38 = (s32[1,3]{1,0:T(1,128)S(1)}, s32[1,3]{1,0:T(1,128)}, u32[]{:S(2)}) copy-start(s32[1,3]{1,0:T(1,128)} %param.7) | copy-start | bytes 40
  4.5 5.1 %collective-permute-start.1 = (bf16[2,1,8,16,128]{4,1,3,2,0:T(2,128)(2,1)S(1)}, bf16[2,1,8,16,128]{4,1,3,2,0:T(2,128)(2,1)S(1)}, u32[]{:S(2)}, u32[]{:S(2)}) collective-permute-start(bf16[2,1,8,16,128]{4,1,3,2,0:T(2,128)(2,1)S(1)} %get-tuple-element.7), channel_id=1, source_target_pairs={{6,0},{12,6},{18,12},{24,18},{30,24},{36,30},{42,36},{48,42},{54,4... | collective-permute-start | bytes 196616 | tf_op jit(solution)/shard_map/ppermute | solution.py:19
  6.5 14.2 %collective-permute-start = (bf16[2,1,8,16,128]{4,1,3,2,0:T(2,128)(2,1)S(1)}, bf16[2,1,8,16,128]{4,1,3,2,0:T(2,128)(2,1)S(1)}, u32[]{:S(2)}, u32[]{:S(2)}) collective-permute-start(bf16[2,1,8,16,128]{4,1,3,2,0:T(2,128)(2,1)S(1)} %get-tuple-element.6), channel_id=1, source_target_pairs={{0,6},{6,12},{12,18},{18,24},{24,30},{30,36},{36,42},{42,48},{48,5... | collective-permute-start | bytes 196616 | tf_op jit(solution)/shard_map/ppermute | solution.py:18
  8.9 12.3 %copy-start.35 = (f32[3]{0:T(128)}, f32[3]{0:T(128)S(1)}, u32[]{:S(2)}) copy-start(f32[3]{0:T(128)S(1)} %fusion.228) | copy-start | bytes 40
  23.7 1.0 copy-start.34
  23.7 1.1 copy-start.33
  23.7 1.1 copy-start.32
  23.7 1.1 copy-start.31
  23.7 1.1 copy-start.30
  23.7 1.2 copy-start.29
  23.7 1.2 copy-start.28
  24.7 1.3 copy-start
  27.9 2.5 %copy-start.1 = (bf16[27,128,128]{2,1,0:T(8,128)(2,1)S(1)}, bf16[27,128,128]{2,1,0:T(8,128)(2,1)}, u32[]{:S(2)}) copy-start(bf16[27,128,128]{2,1,0:T(8,128)(2,1)} %param.8) | copy-start | bytes 2654212
  32.0 2.2 %copy-start.37 = (f32[192]{0:T(256)S(1)}, f32[192]{0:T(256)}, u32[]{:S(2)}) copy-start(f32[192]{0:T(256)} %mul.127) | copy-start | bytes 2308
  34.6 19.4 %copy-start.36 = (f32[3]{0:T(128)S(1)}, f32[3]{0:T(128)}, u32[]{:S(2)}) copy-start(f32[3]{0:T(128)} %copy-done.35) | copy-start | bytes 40
  55.5 18.6 %collective-permute-start.5 = (bf16[1,8,16,128]{3,0,2,1:T(2,128)(2,1)}, bf16[1,8,16,128]{3,0,2,1:T(2,128)(2,1)}, u32[]{:S(2)}, u32[]{:S(2)}) collective-permute-start(bf16[1,8,16,128]{3,0,2,1:T(2,128)(2,1)} %copy.477), channel_id=1, source_target_pairs={{6,0},{12,6},{18,12},{24,18},{30,24},{36,30},{42,36},{48,42},{54,4... | collective-permute-start | bytes 98312 | tf_op jit(solution)/shard_map/ppermute | solution.py:19
  58.2 16.0 %collective-permute-start.4 = (bf16[1,8,16,128]{3,0,2,1:T(2,128)(2,1)}, bf16[1,8,16,128]{3,0,2,1:T(2,128)(2,1)}, u32[]{:S(2)}, u32[]{:S(2)}) collective-permute-start(bf16[1,8,16,128]{3,0,2,1:T(2,128)(2,1)} %copy.474), channel_id=1, source_target_pairs={{0,6},{6,12},{12,18},{18,24},{24,30},{30,36},{36,42},{42,48},{48,5... | collective-permute-start | bytes 98312 | tf_op jit(solution)/shard_map/ppermute | solution.py:18
  62.1 17.4 %collective-permute-start.3 = (bf16[1,8,16,128]{3,0,2,1:T(2,128)(2,1)}, bf16[1,8,16,128]{3,0,2,1:T(2,128)(2,1)}, u32[]{:S(2)}, u32[]{:S(2)}) collective-permute-start(bf16[1,8,16,128]{3,0,2,1:T(2,128)(2,1)} %copy.418), channel_id=1, source_target_pairs={{6,0},{12,6},{18,12},{24,18},{30,24},{36,30},{42,36},{48,42},{54,4... | collective-permute-start | bytes 98312 | tf_op jit(solution)/shard_map/ppermute | solution.py:19
  66.0 13.5 %collective-permute-start.2 = (bf16[1,8,16,128]{3,0,2,1:T(2,128)(2,1)}, bf16[1,8,16,128]{3,0,2,1:T(2,128)(2,1)}, u32[]{:S(2)}, u32[]{:S(2)}) collective-permute-start(bf16[1,8,16,128]{3,0,2,1:T(2,128)(2,1)} %copy.415), channel_id=1, source_target_pairs={{0,6},{6,12},{12,18},{18,24},{24,30},{30,36},{36,42},{42,48},{48,5... | collective-permute-start | bytes 98312 | tf_op jit(solution)/shard_map/ppermute | solution.py:18
  81.4 3.0 %copy-start.4 = (bf16[3,4,4,4,128]{4,1,3,2,0:T(4,128)(2,1)S(1)}, bf16[3,4,4,4,128]{4,1,3,2,0:T(4,128)(2,1)}, u32[]{:S(2)}) copy-start(bf16[3,4,4,4,128]{4,1,3,2,0:T(4,128)(2,1)} %get-tuple-element.32) | copy-start | bytes 147460
  81.4 3.0 %copy-start.3 = (bf16[3,4,4,4,128]{4,1,3,2,0:T(4,128)(2,1)S(1)}, bf16[3,4,4,4,128]{4,1,3,2,0:T(4,128)(2,1)}, u32[]{:S(2)}) copy-start(bf16[3,4,4,4,128]{4,1,3,2,0:T(4,128)(2,1)} %get-tuple-element.31) | copy-start | bytes 147460
  83.0 0.8 copy-start.6
  83.0 1.2 copy-start.2
  83.0 1.3 copy-start.5
  83.0 1.5 copy-start.27
  83.0 1.6 copy-start.26
  83.0 1.6 copy-start.25
  83.0 1.6 copy-start.24
  83.0 1.7 copy-start.23
  83.0 1.7 copy-start.22
  83.0 1.7 copy-start.21
  83.1 1.7 copy-start.20
  83.1 1.8 copy-start.19
  83.1 1.8 copy-start.18
  83.2 1.7 copy-start.17
  83.2 1.7 copy-start.16
  83.2 1.8 copy-start.15
  83.2 1.8 copy-start.14
  83.2 1.8 copy-start.13
  83.3 1.9 copy-start.12
  83.3 1.9 copy-start.11
  83.3 1.9 copy-start.10
  83.3 1.9 copy-start.9
  92.1 2.2 %copy-start.7 = (bf16[1,3,64,128]{3,2,1,0:T(8,128)(2,1)S(1)}, bf16[1,3,64,128]{3,2,1,0:T(8,128)(2,1)}, u32[]{:S(2)}) copy-start(bf16[1,3,64,128]{3,2,1,0:T(8,128)(2,1)} %param.6) | copy-start | bytes 147460
  92.1 2.2 %copy-start.8 = (bf16[1,3,64,128]{3,2,1,0:T(8,128)(2,1)S(1)}, bf16[1,3,64,128]{3,2,1,0:T(8,128)(2,1)}, u32[]{:S(2)}) copy-start(bf16[1,3,64,128]{3,2,1,0:T(8,128)(2,1)} %param.5) | copy-start | bytes 147460
  122.8 4.8 %collective-permute-start.6 = (bf16[4,8,2,54,128]{4,0,1,2,3:T(4,128)(2,1)}, bf16[4,8,2,54,128]{4,0,1,2,3:T(4,128)(2,1)}, u32[]{:S(2)}, u32[]{:S(2)}) collective-permute-start(bf16[4,8,2,54,128]{4,0,1,2,3:T(4,128)(2,1)} %copy.506), channel_id=1, source_target_pairs={{0,6},{6,0},{1,7},{7,1},{2,8},{8,2},{3,9},{9,3},{4,10},{10,4},{5,1... | collective-permute-start | bytes 2654216 | tf_op jit(solution)/shard_map/ppermute | solution.py:113

commit v2 on v0

v2 whole, which is shorter than its diff:
```python
import jax
import jax.numpy as jnp
from jax import lax
from jax.experimental import pallas as pl
from jax.experimental.pallas import tpu as pltpu
from jax.sharding import Mesh, PartitionSpec as P

BY = 2
BZ = 4
C = 128
SLOTS = 3
TILE = ("zh", "y", "x", "c")
SCENE = ("sa", "sb")
F32 = jnp.float32
BF16 = jnp.bfloat16


def fetch(pairs, sems):
    copies = [pltpu.make_async_copy(src, dst, sems.at[k]) for k, (src, dst) in enumerate(pairs)]
    for copy in copies:
        copy.start()
    return copies


def halo_kernel(blocks, features, cotangent, outer, inner, ids, sems):
    core = lax.axis_index("c")
    edge = pl.ds(pl.multiple_of(32 * core, 32), 32)
    copies = fetch(
        [
            (blocks, ids),
            (features.at[0, :, edge, :], outer.at[0, 0:3]),
            (cotangent.at[0, :, edge, :], outer.at[0, 3:6]),
            (features.at[0], inner.at[0:3]),
            (cotangent.at[0], inner.at[3:6]),
        ],
        sems,
    )
    copies[0].wait()
    row = lax.broadcasted_iota(jnp.int32, (32, C), 0)
    marks = jnp.zeros((32, C), F32)
    for j in range(SLOTS):
        marks = jnp.where(row == j, (ids[0, j] + 1).astype(F32), marks)
    outer[0, 6] = marks.astype(BF16)
    inner[6, 0:32] = marks.astype(BF16)
    inner[6, 32:64] = jnp.zeros((32, C), BF16)
    for copy in copies[1:]:
        copy.wait()


def block_masks(ids):
    upper = lax.broadcasted_iota(jnp.int32, (8, C), 0) // 4
    return [
        [[ids[j] == (upper + (4 * by + 2 * h)) for h in range(2)] for by in range(BY)]
        for j in range(SLOTS)
    ]


def live_tiles(masks):
    rows = []
    for by in range(BY):
        halves = []
        for h in range(2):
            any_slot = masks[0][by][h] | masks[1][by][h] | masks[2][by][h]
            halves.append(jnp.where(any_slot, 1.0, 0.0))
        tile = jnp.concatenate(halves, axis=0)
        rows.append(jnp.broadcast_to(tile[None], (4, 16, C)))
    return jnp.concatenate(rows, axis=0)


def to_slab(rows, masks, layers):
    count = SLOTS * layers * 16
    low = lax.broadcasted_iota(jnp.int32, (count, C), 0) % 8 < 4
    even = jnp.where(low, rows, pltpu.roll(rows, 4, 0))
    odd = jnp.where(low, pltpu.roll(rows, count - 4, 0), rows)
    shape = (SLOTS, layers, 2, 8, C)
    even, odd = even.reshape(shape), odd.reshape(shape)
    whole = []
    for by in range(BY):
        halves = []
        for h in range(2):
            pair = []
            for part in (even, odd):
                picked = jnp.zeros((layers, 2, 8, C), F32)
                for j in range(SLOTS):
                    picked = jnp.where(masks[j][by][h][None, None], part[j], picked)
                pair.append(picked)
            halves.append(jnp.stack(pair, axis=2).reshape(layers, 4, 8, C))
        whole.append(jnp.concatenate(halves, axis=2))
    return jnp.concatenate(whole, axis=1)


def from_slab(slab, masks, layers):
    low = lax.broadcasted_iota(jnp.int32, (8, C), 0) < 4
    slots = []
    for j in range(SLOTS):
        picked = jnp.zeros((layers, 4, 8, C), F32)
        for by in range(BY):
            for h in range(2):
                part = slab[:, 4 * by : 4 * by + 4, 8 * h : 8 * h + 8, :]
                picked = picked + jnp.where(masks[j][by][h][None, None], part, 0.0)
        flat = picked.reshape(layers * 32, C)
        both = (flat + pltpu.roll(flat, 4, 0)).reshape(layers, 2, 2, 8, C)
        rest = (flat + pltpu.roll(flat, layers * 32 - 4, 0)).reshape(layers, 2, 2, 8, C)
        full_even = rest[:, :, 0]
        full_odd = both[:, :, 1]
        slots.append(jnp.where(low[None, None], full_even, full_odd).reshape(layers * 16, C))
    return jnp.stack(slots)


def shifted_rows(slab, layers):
    flat = slab.reshape(layers * 128, C)
    z = lax.broadcasted_iota(jnp.int32, (layers * 128, C), 0) % 16
    before = jnp.where(z == 0, 0.0, pltpu.roll(flat, 1, 0))
    after = jnp.where(z == 15, 0.0, pltpu.roll(flat, layers * 128 - 1, 0))
    return before, flat, after


def store_shifted(out, slab, layers):
    for c, rows in enumerate(shifted_rows(slab, layers)):
        out[c, :, 1:9] = rows.astype(BF16).reshape(layers, 8, 16, C)
        out[c, :, 0] = jnp.zeros((layers, 16, C), BF16)
        out[c, :, 9] = jnp.zeros((layers, 16, C), BF16)


def taps(shifted, weights, layers):
    lhs = jnp.concatenate(
        [shifted[c, :, b : b + 8].reshape(layers * 128, C) for b in range(3) for c in range(3)], axis=1
    )
    rhs = jnp.concatenate([weights[9 * a : 9 * a + 9].reshape(9 * C, C) for a in range(3)], axis=1)
    return jnp.dot(lhs, rhs, preferred_element_type=F32).reshape(layers, 128, 3 * C)


def taps_back(shifted, weights, layers):
    lhs = jnp.concatenate(
        [shifted[2 - c, :, 2 - b : 10 - b].reshape(layers * 128, C) for b in range(3) for c in range(3)], axis=1
    )
    rhs = jnp.concatenate(
        [jnp.concatenate([weights[9 * (2 - a) + k] for k in range(9)], axis=1) for a in range(3)], axis=0
    )
    out = lax.dot_general(lhs, rhs, (((1,), (1,)), ((), ())), preferred_element_type=F32)
    return out.reshape(layers, 128, 3 * C)


def thirds(out):
    return out[:, :, 0:C], out[:, :, C : 2 * C], out[:, :, 2 * C : 3 * C]


def inside(out, layers):
    after, same, before = thirds(out)
    n = layers - 2
    return after[0:n] + same[1 : n + 1] + before[2 : n + 2]


def spread(out):
    after, same, before = thirds(out)
    none = jnp.zeros((1, 128, C), F32)
    return (
        jnp.concatenate([none, none, after], axis=0)
        + jnp.concatenate([none, same, none], axis=0)
        + jnp.concatenate([before, none, none], axis=0)
    )


def completed(part, out):
    after, same, before = thirds(out)
    return jnp.concatenate(
        [
            part[0:1] + after[0:1] + same[1:2],
            part[1:2] + after[1:2],
            part[2:8],
            part[8:9] + before[2:3],
            part[9:10] + same[2:3] + before[3:4],
        ],
        axis=0,
    )


def weight_terms(order, shifted_layers, padded, terms):
    turned = jnp.concatenate(
        [
            lax.dot_general(order, rows, (((1,), (1,)), ((), ())), preferred_element_type=F32).astype(BF16)
            for rows in shifted_layers
        ],
        axis=0,
    )
    rhs = jnp.concatenate([padded(a, b) for a in range(3) for b in range(3)], axis=1)
    out = jnp.dot(turned, rhs, preferred_element_type=F32)
    for a in range(3):
        for b in range(3):
            for c in range(3):
                piece = out[c * C : (c + 1) * C, (3 * a + b) * C : (3 * a + b + 1) * C]
                half, tap = divmod(9 * a + 3 * b + c, 14)
                terms[:, half, tap] = piece.astype(BF16).reshape(4, 32, C)
    terms[:, 1, 13] = jnp.zeros((4, 32, C), BF16)


def pad_store(out, slab):
    out[0:2] = jnp.zeros((2, 10, 16, C), BF16)
    out[10:12] = jnp.zeros((2, 10, 16, C), BF16)
    out[2:10, 0] = jnp.zeros((8, 16, C), BF16)
    out[2:10, 9] = jnp.zeros((8, 16, C), BF16)
    out[2:10, 1:9] = slab.astype(BF16)


def ids_of(tile):
    rows = tile.astype(F32).astype(jnp.int32)
    return [jnp.broadcast_to(rows[j : j + 1] - 1, (8, C)) for j in range(SLOTS)]


def choose(even, one, other):
    return [jnp.where(even, p, q) for p, q in zip(one, other)]


def chip_ids(own, partner, even):
    own, partner = ids_of(own[6, 0:16]), ids_of(partner[6, 0:16])
    return choose(even, own, partner), choose(even, partner, own)


def chip_kernel(
    own, partner, w_first_hbm, w_second_hbm,
    w_first, w_second, field_z, upstream_pad, act_part, grad_part,
    upstream_z, sems,
):
    copies = fetch([(w_first_hbm, w_first), (w_second_hbm, w_second)], sems)
    even = lax.axis_index("c") == 0
    masks = [block_masks(ids) for ids in chip_ids(own, partner, even)]

    def field(which):
        partner_rows = partner[3 * which : 3 * which + 3].astype(F32).reshape(192, C)
        own_rows = own[3 * which : 3 * which + 3].astype(F32).reshape(192, C)
        parts = (
            to_slab(jnp.where(even, own_rows, partner_rows), masks[0], 4),
            to_slab(jnp.where(even, partner_rows, own_rows), masks[1], 4),
        )
        return jnp.concatenate(parts, axis=0)

    store_shifted(field_z, field(0), 8)
    upstream = field(1)
    store_shifted(upstream_z, upstream, 8)
    pad_store(upstream_pad, upstream)
    copies[0].wait()
    act_part[...] = spread(taps(field_z, w_first, 8))
    copies[1].wait()
    grad_part[...] = spread(taps_back(upstream_z, w_second, 8))


def main_kernel(
    own, partner, far, near, w_first, w_second, field_z, upstream_pad, act_part, grad_part,
    terms, hidden_out, grad_out,
    outer_z, outer_up_z, stage_z, padded,
):
    core = lax.axis_index("c")
    even = core == 0
    near_ids, far_ids = ids_of(near[0, 6, 0:16]), ids_of(far[0, 6, 0:16])
    left, right = (block_masks(ids) for ids in (choose(even, near_ids, far_ids), choose(even, far_ids, near_ids)))
    lower, upper = (block_masks(ids) for ids in chip_ids(own, partner, even))

    def field(which):
        near_rows = near[0, 3 * which : 3 * which + 3].astype(F32).reshape(96, C)
        far_rows = far[0, 3 * which : 3 * which + 3].astype(F32).reshape(96, C)
        parts = (
            to_slab(jnp.where(even, near_rows, far_rows), left, 2),
            to_slab(jnp.where(even, far_rows, near_rows), right, 2),
        )
        return jnp.concatenate(parts, axis=0)

    store_shifted(outer_z, field(0), 4)
    store_shifted(outer_up_z, field(1), 4)
    first_act = completed(act_part[...], taps(outer_z, w_first, 4)).reshape(10, 8, 16, C)
    live = jnp.concatenate(
        [
            live_tiles(left)[None],
            jnp.broadcast_to(live_tiles(lower)[None], (4, 8, 16, C)),
            jnp.broadcast_to(live_tiles(upper)[None], (4, 8, 16, C)),
            live_tiles(right)[None],
        ],
        axis=0,
    )
    gate = 1.0 / (1.0 + jnp.exp(-first_act))
    hidden = live * (first_act * gate)
    hidden_out[...] = hidden.astype(BF16)
    slope = live * (gate * (1.0 + first_act * (1.0 - gate)))
    hidden_grad = completed(grad_part[...], taps_back(outer_up_z, w_second, 4)).reshape(10, 8, 16, C)
    grad_out[...] = (hidden_grad * slope).astype(BF16)

    @pl.when(even)
    def _():
        for c in range(3):
            stage_z[c, 0] = outer_z[c, 1, 1:9]
            stage_z[c, 1:9] = field_z[c, :, 1:9]
            stage_z[c, 9] = outer_z[c, 2, 1:9]
        pad_store(padded, grad_out[1:9])

    @pl.when(core == 1)
    def _():
        for c, rows in enumerate(shifted_rows(hidden_out[...].astype(F32), 10)):
            stage_z[c] = rows.astype(BF16).reshape(10, 8, 16, C)
        padded[...] = upstream_pad[...]

    r = lax.broadcasted_iota(jnp.int32, (C, C), 0)
    i = lax.broadcasted_iota(jnp.int32, (C, C), 1)
    wanted = (((r // 2) % 2 * 8 + (r // 4) % 8) * 4 + r // 32) * 2 + r % 2
    order = jnp.where(i == wanted, 1.0, 0.0).astype(BF16)
    weight_terms(
        order,
        [stage_z[c].reshape(1280, C) for c in range(3)],
        lambda a, b: padded[2 - a : 12 - a, 2 - b : 10 - b].reshape(1280, C),
        terms,
    )


def output_kernel(
    blocks, features, cotangent, hidden, first_grad, w_first, w_second,
    block_out, input_grad,
    hidden_z, grad_z,
):
    mine = pl.ds(4 * lax.axis_index("c"), 6)
    own = block_masks([blocks[0, j] for j in range(SLOTS)])
    store_shifted(hidden_z, hidden[mine].astype(F32), 6)
    store_shifted(grad_z, first_grad[mine].astype(F32), 6)
    second_act = from_slab(inside(taps(hidden_z, w_second, 6), 6).reshape(4, 8, 16, C), own, 4)
    back = from_slab(inside(taps_back(grad_z, w_first, 6), 6).reshape(4, 8, 16, C), own, 4)
    for j in range(SLOTS):
        live = jnp.where(blocks[0, j] < BY * BZ, 1.0, 0.0)
        block_out[0, j] = (live * (features[0, j].astype(F32) + second_act[j])).astype(BF16)
        input_grad[0, j] = (live * (cotangent[0, j].astype(F32) + back[j])).astype(BF16)


VMEM = pl.BlockSpec(memory_space=pltpu.VMEM)
SMEM = pl.BlockSpec(memory_space=pltpu.SMEM)
HBM = pl.BlockSpec(memory_space=pltpu.HBM)


def kernel_call(body, ins, outs, scratch, flops, room=50):
    return pl.pallas_call(
        body,
        out_shape=outs,
        in_specs=ins,
        out_specs=[VMEM] * len(outs),
        scratch_shapes=scratch,
        compiler_params=pltpu.CompilerParams(vmem_limit_bytes=room * 1024 * 1024),
        cost_estimate=pl.CostEstimate(flops=flops, bytes_accessed=4_000_000, transcendentals=0),
    )


def shape(*dims, dtype=BF16):
    return jax.ShapeDtypeStruct(dims, dtype)


def folded(pieces):
    return pieces.astype(F32).sum(axis=0)


def on_device(features, cotangent, blocks, w_first, w_second):
    outer, inner = kernel_call(
        halo_kernel,
        [HBM] * 3,
        [shape(1, 7, 32, C), shape(7, 64, C)],
        [pltpu.SMEM((1, SLOTS), jnp.int32), pltpu.SemaphoreType.DMA((5,))],
        1,
        64,
    )(blocks, features, cotangent)
    odd = range(1, 127, 2)
    partner = lax.ppermute(inner, "c", [(0, 1), (1, 0)])
    far = lax.ppermute(outer, TILE, [(t + 2, t) for t in range(0, 126, 2)] + [(t, t + 2) for t in range(1, 126, 2)])
    near = lax.ppermute(outer, TILE, [(t, t + 1) for t in odd] + [(t + 1, t) for t in odd])
    w_first, w_second, field_z, upstream_pad, act_part, grad_part = kernel_call(
        chip_kernel,
        [VMEM, VMEM, HBM, HBM],
        [
            shape(27, C, C),
            shape(27, C, C),
            shape(3, 8, 10, 16, C),
            shape(12, 10, 16, C),
            shape(10, 128, C, dtype=F32),
            shape(10, 128, C, dtype=F32),
        ],
        [pltpu.VMEM((3, 8, 10, 16, C), BF16), pltpu.SemaphoreType.DMA((2,))],
        2_000_000_000,
        40,
    )(inner, partner, w_first, w_second)
    terms, hidden, first_grad = kernel_call(
        main_kernel,
        [VMEM] * 10,
        [shape(4, 2, 14, 32, C), shape(10, 8, 16, C), shape(10, 8, 16, C)],
        [
            pltpu.VMEM((3, 4, 10, 16, C), BF16),
            pltpu.VMEM((3, 4, 10, 16, C), BF16),
            pltpu.VMEM((3, 10, 8, 16, C), BF16),
            pltpu.VMEM((12, 10, 16, C), BF16),
        ],
        2_000_000_000,
        40,
    )(inner, partner, far, near, w_first, w_second, field_z, upstream_pad, act_part, grad_part)
    block_out, input_grad = kernel_call(
        output_kernel,
        [SMEM] + [VMEM] * 6,
        [shape(1, SLOTS, 64, C)] * 2,
        [pltpu.VMEM((3, 6, 10, 16, C), BF16), pltpu.VMEM((3, 6, 10, 16, C), BF16)],
        1_400_000_000,
    )(blocks, features, cotangent, hidden, first_grad, w_first, w_second)
    terms = terms.reshape(8, 14, 32, C)
    along_x = folded(lax.all_to_all(terms, ("x", "sb"), 0, 0, tiled=True)).reshape(14, 8, 4, C)
    along_y = folded(lax.all_to_all(along_x.transpose(1, 2, 0, 3), "y", 0, 0, tiled=True)).astype(BF16)
    copies = jnp.broadcast_to(along_y[:, None], (4, 6, 14, C)).reshape(24, 14, C)
    pieces = lax.all_to_all(copies, ("zh", "c", "sa", "sb"), 0, 0, tiled=True).reshape(2, 2, 3, 2, 14, C)
    total = pieces.astype(F32).sum(axis=(0, 2)).reshape(2, 28, C)
    return block_out, input_grad, total[0, :27], total[1, :27]


def solution(mesh):
    split = Mesh(mesh.devices.reshape(2, 8, 4, 2, 3, 2), TILE + SCENE)
    return jax.shard_map(
        on_device,
        mesh=split,
        in_specs=(
            P(SCENE, TILE, None, None),
            P(SCENE, TILE, None, None),
            P(SCENE, TILE),
            P(),
            P(),
        ),
        out_specs=(
            P(SCENE, TILE, None, None),
            P(SCENE, TILE, None, None),
            P(None, TILE),
            P(None, TILE),
        ),
        check_vma=False,
    )
```

time: 2090 us -> 88.2 us (0.04)
  waiting for transfers between devices: 1940 us -> 8.17 us
  matrix products: 32 us -> 0 us
  local copies, waits for them, and re-layouts: 27.4 us -> 4.63 us
    reduce_scatter x2 -> x0, waiting for transfers between devices: 1940 us -> none  [the longest x1 974 us: on_device(): lax.psum_scatter(first_terms, 'tile', scatter_dimension=1, tiled=True)]
    all_to_all x0 -> x2, blocking collectives: none -> 34.3 us  [the longest x1 20.8 us: on_device(): lax.all_to_all(along_x.transpose(1, 2, 0, 3), 'y', 0, 0, tiled=True)]
    dot_general x162 -> x0, matrix products: 32 us -> none  [the longest x54 16.1 us: weight_terms(): lax.dot_general(window_piece.reshape(-1, channels), gradient_rows, (((0,)...]
    psum x1 -> x0, blocking collectives: 28 us -> none  [on_device(): first_total, second_total = lax.psum((first_share, second_share), 'scene')]
  transfers between devices with their start and end apart: 8 -> 4, of which waited for: 3 -> 1; matrix products, arithmetic and copies ran while one was open for 2% -> 0% of each run, Pallas kernels for 0% -> 8%
where the time goes in v2:
time: 88.2 us; the launch traced here: 87.7 us
  blocking collectives  34.3 us (39%)
  starting transfers between devices  26.5 us (30%)
  Pallas kernels  13.1 us (15%)
  waiting for transfers between devices  8.17 us (9%)
  local copies, waits for them, and re-layouts  4.63 us (5%)
    all_to_all x1, blocking collectives, on_device(): lax.all_to_all(along_x.transpose(1, 2, 0, 3), 'y', 0, 0, tiled=True)  20.8 us
    all_to_all x1, blocking collectives, on_device(): lax.all_to_all(terms, ('x', 'sb'), 0, 0, tiled=True)  13.4 us
    ppermute x1, starting transfers between devices, on_device(): partner = lax.ppermute(inner, 'c', [(0, 1), (1, 0)])  12.4 us
    all_to_all x1, starting transfers between devices, on_device(): lax.all_to_all(copies, ('zh', 'c', 'sa', 'sb'), 0, 0, tiled=True)  10.9 us
    all_to_all x1, waiting for transfers between devices, on_device(): lax.all_to_all(copies, ('zh', 'c', 'sa', 'sb'), 0, 0, tiled=True)  8.16 us
    pallas_call x1, Pallas kernels, on_device(): kernel_call(chip_kernel, [VMEM, VMEM, HBM, HBM], [shape(27, C, C), shape(...  4.12 us
    pallas_call x1, Pallas kernels, on_device(): kernel_call(main_kernel, [VMEM] * 10, [shape(4, 2, 14, 32, C), shape(10,...  4.02 us
    unnamed x15, local copies, waits for them, and re-layouts  3.86 us
  transfers between devices with their start and end apart: 4, of which 1 were waited for; matrix products, arithmetic and copies ran while one was open for 0% of the time, Pallas kernels for 8%

profile of v2, /device:TPU:1, one launch (start us, length us, event | category | flops | bytes accessed | tf_op | source)
XLA Modules:
  0.0 87.7 jit_solution(985760700729050972)
XLA Ops:
  0.6 1.6 %shard_map.84 = (bf16[1,7,32,128]{3,2,1,0:T(8,128)(2,1)}, bf16[7,64,128]{2,1,0:T(8,128)(2,1)}) custom-call(s32[1,3]{1,0:T(1,128)} %blocks.3, bf16[1,3,64,128]{3,2,1,0:T(8,128)(2,1)} %features.3, bf16[1,3,64,128]{3,2,1,0:T(8,128)(2,1)} %cotangent.3), custom_call_target="tpu_custom_call" | custom-call | flops 1 | bytes 4000000 | tf_op jit(solution)/shard_map/pallas_call | solution.py:355
  2.2 12.4 %collective-permute-start = (bf16[7,64,128]{2,1,0:T(8,128)(2,1)}, bf16[7,64,128]{2,1,0:T(8,128)(2,1)S(1)}, u32[]{:S(2)}, u32[]{:S(2)}) collective-permute-start(bf16[7,64,128]{2,1,0:T(8,128)(2,1)} %get-tuple-element.17.own), channel_id=1, source_target_pairs={{0,6},{6,0},{1,7},{7,1},{2,8},{8,2},{3,9},{9,3},{4,10},{10,4},{5,1... | collective-permute-start | bytes 344072 | tf_op jit(solution)/shard_map/ppermute | solution.py:364
  14.7 1.9 %collective-permute-start.2 = (bf16[1,7,32,128]{3,2,1,0:T(8,128)(2,1)}, bf16[1,7,32,128]{3,2,1,0:T(8,128)(2,1)S(1)}, u32[]{:S(2)}, u32[]{:S(2)}) collective-permute-start(bf16[1,7,32,128]{3,2,1,0:T(8,128)(2,1)} %get-tuple-element.18), channel_id=1, source_target_pairs={{6,12},{18,24},{30,36},{42,48},{54,60},{66,72},{78,84},{90,96},{10... | collective-permute-start | bytes 172040 | tf_op jit(solution)/shard_map/ppermute | solution.py:366
  16.6 1.3 %collective-permute-start.1 = (bf16[1,7,32,128]{3,2,1,0:T(8,128)(2,1)}, bf16[1,7,32,128]{3,2,1,0:T(8,128)(2,1)S(1)}, u32[]{:S(2)}, u32[]{:S(2)}) collective-permute-start(bf16[1,7,32,128]{3,2,1,0:T(8,128)(2,1)} %get-tuple-element.18), channel_id=1, source_target_pairs={{12,0},{24,12},{36,24},{48,36},{60,48},{72,60},{84,72},{96,84},{10... | collective-permute-start | bytes 172040 | tf_op jit(solution)/shard_map/ppermute | solution.py:365
  17.9 0.0 collective-permute-done.partner
  17.9 0.0 copy-start.3
  17.9 1.2 %copy-done.3 = bf16[27,128,128]{2,1,0:T(8,128)(2,1)S(1)} copy-done((bf16[27,128,128]{2,1,0:T(8,128)(2,1)S(1)}, bf16[27,128,128]{2,1,0:T(8,128)(2,1)}, u32[]{:S(2)}) %copy-start.3) | copy-done | bytes 884760
  19.1 0.0 copy-start.4
  19.1 1.2 %copy-done.4 = bf16[27,128,128]{2,1,0:T(8,128)(2,1)S(1)} copy-done((bf16[27,128,128]{2,1,0:T(8,128)(2,1)S(1)}, bf16[27,128,128]{2,1,0:T(8,128)(2,1)}, u32[]{:S(2)}) %copy-start.4) | copy-done | bytes 884760
  20.2 0.0 copy-start.5
  20.2 0.9 %copy-done.5 = bf16[7,64,128]{2,1,0:T(8,128)(2,1)S(1)} copy-done((bf16[7,64,128]{2,1,0:T(8,128)(2,1)S(1)}, bf16[7,64,128]{2,1,0:T(8,128)(2,1)}, u32[]{:S(2)}) %copy-start.5) | copy-done | bytes 114712
  21.1 0.0 copy-start.6
  21.1 4.1 %shard_map.85 = (bf16[27,128,128]{2,1,0:T(8,128)(2,1)S(1)}, bf16[27,128,128]{2,1,0:T(8,128)(2,1)S(1)}, bf16[3,8,10,16,128]{4,3,2,1,0:T(8,128)(2,1)S(1)}, bf16[12...) custom-call(bf16[7,64,128]{2,1,0:T(8,128)(2,1)S(1)} %copy-done.5, ...), custom_call_target="tpu_custom_call" | custom-call | flops 2000000000 | bytes 4000000 | tf_op jit(solution)/shard_map/pallas_call | solution.py:367
  25.3 0.0 collective-permute-done.2.near
  25.3 0.0 collective-permute-done.1.far
  25.3 0.0 copy-done.6
  25.3 4.0 %shard_map.86 = (bf16[4,2,14,32,128]{4,3,2,1,0:T(8,128)(2,1)S(1)}, bf16[10,8,16,128]{3,2,1,0:T(8,128)(2,1)S(1)}, bf16[10,8,16,128]{3,2,1,0:T(8,128)(2,1)S(1)}) custom-call(bf16[7,64,128]{2,1,0:T(8,128)(2,1)S(1)} %copy-done.6, bf16[7,64,128]{2,1,0:T(8,128)(2,1)S(1)} %collective-permute-done.partner, bf16[1,7,32,128]{3,2,1,0:T(8,128)(2,1)S(1)} %collective-permute-done.1.far, ...), custom_call_target="tpu_custom_call" | custom-call | flops 2000000000 | bytes 4000000 | tf_op jit(solution)/shard_map/pallas_call | solution.py:382
  29.3 13.4 %all_to_all.15 = bf16[8,14,32,128]{3,2,1,0:T(8,128)(2,1)S(1)} all-to-all(bf16[8,14,32,128]{3,2,1,0:T(8,128)(2,1)S(1)} %bitcast.12), channel_id=1, replica_groups=mesh['zh'=2,'y'=8,'x'=4,'c'=2,'sa'=3,'sb'=2] {'x','sb'}, dimensions={0} | all-to-all | bytes 1835008 | tf_op jit(solution)/shard_map/all_to_all | solution.py:403
  42.8 0.1 convert_reduce_fusion
  42.9 0.0 copy-start
  42.9 0.0 copy-start.1
  42.9 0.0 copy-start.2
  43.0 20.8 %all_to_all.16 = f32[8,4,14,128]{3,1,2,0:T(4,128)S(1)} all-to-all(f32[8,4,14,128]{3,1,2,0:T(4,128)S(1)} %copy.28), channel_id=1, replica_groups=mesh['zh'=2,'y'=8,'x'=4,'c'=2,'sa'=3,'sb'=2] {'y'}, dimensions={0} | all-to-all | bytes 458752 | tf_op jit(solution)/shard_map/all_to_all | solution.py:404
  63.9 0.7 broadcast_in_dim.2
  64.5 10.9 %all-to-all-start.2 = ((bf16[24,14,128]{2,1,0:T(8,128)(2,1)}), bf16[24,14,128]{2,1,0:T(8,128)(2,1)S(1)}, u32[]{:S(2)}, u32[]{:S(2)}) async-start(bf16[24,14,128]{2,1,0:T(8,128)(2,1)} %bitcast.3), calls=%async_computation.2 | async-start | bytes 196608 | tf_op jit(solution)/shard_map/all_to_all | solution.py:406
  75.4 0.0 copy-done
  75.4 0.0 copy-done.1
  75.4 0.0 copy-done.2
  75.4 3.3 %shard_map.87 = (bf16[1,3,64,128]{3,2,1,0:T(8,128)(2,1)}, bf16[1,3,64,128]{3,2,1,0:T(8,128)(2,1)}) custom-call(s32[1,3]{1,0:T(1,128)S(1)} %copy-done.2, bf16[1,3,64,128]{3,2,1,0:T(8,128)(2,1)S(1)} %copy-done, bf16[1,3,64,128]{3,2,1,0:T(8,128)(2,1)S(1)} %copy-done.1, bf16[10,8,16,128]{3,2,1,0:T(8,128)(2,1)S(1)} %get-tuple-element.25.hidden, ...), custom_call_target="tpu_custom_call" | custom-call | flops 1400000000 | bytes 4000000 | tf_op jit(solution)/shard_map/pallas_call | solution.py:395
  78.7 8.2 %all-to-all-done.2 = bf16[24,14,128]{2,1,0:T(8,128)(2,1)S(1)} async-done(((bf16[24,14,128]{2,1,0:T(8,128)(2,1)}), bf16[24,14,128]{2,1,0:T(8,128)(2,1)S(1)}, u32[]{:S(2)}, u32[]{:S(2)}) %all-to-all-start.2) | async-done | bytes 86048 | tf_op jit(solution)/shard_map/all_to_all | solution.py:406
  86.9 0.1 convert_reduce_fusion.1
  87.1 0.6 copy_bitcast_fusion
  (6 shorter events, 0.2 us)
Async XLA Ops:
  2.2 15.7 %collective-permute-start = (bf16[7,64,128]{2,1,0:T(8,128)(2,1)}, bf16[7,64,128]{2,1,0:T(8,128)(2,1)S(1)}, u32[]{:S(2)}, u32[]{:S(2)}) collective-permute-start(bf16[7,64,128]{2,1,0:T(8,128)(2,1)} %get-tuple-element.17.own), channel_id=1, source_target_pairs={{0,6},{6,0},{1,7},{7,1},{2,8},{8,2},{3,9},{9,3},{4,10},{10,4},{5,1... | collective-permute-start | bytes 344072 | tf_op jit(solution)/shard_map/ppermute | solution.py:364
  14.7 10.6 %collective-permute-start.2 = (bf16[1,7,32,128]{3,2,1,0:T(8,128)(2,1)}, bf16[1,7,32,128]{3,2,1,0:T(8,128)(2,1)S(1)}, u32[]{:S(2)}, u32[]{:S(2)}) collective-permute-start(bf16[1,7,32,128]{3,2,1,0:T(8,128)(2,1)} %get-tuple-element.18), channel_id=1, source_target_pairs={{6,12},{18,24},{30,36},{42,48},{54,60},{66,72},{78,84},{90,96},{10... | collective-permute-start | bytes 172040 | tf_op jit(solution)/shard_map/ppermute | solution.py:366
  16.6 8.7 %collective-permute-start.1 = (bf16[1,7,32,128]{3,2,1,0:T(8,128)(2,1)}, bf16[1,7,32,128]{3,2,1,0:T(8,128)(2,1)S(1)}, u32[]{:S(2)}, u32[]{:S(2)}) collective-permute-start(bf16[1,7,32,128]{3,2,1,0:T(8,128)(2,1)} %get-tuple-element.18), channel_id=1, source_target_pairs={{12,0},{24,12},{36,24},{48,36},{60,48},{72,60},{84,72},{96,84},{10... | collective-permute-start | bytes 172040 | tf_op jit(solution)/shard_map/ppermute | solution.py:365
  17.9 1.2 %copy-start.3 = (bf16[27,128,128]{2,1,0:T(8,128)(2,1)S(1)}, bf16[27,128,128]{2,1,0:T(8,128)(2,1)}, u32[]{:S(2)}) copy-start(bf16[27,128,128]{2,1,0:T(8,128)(2,1)} %w_first_hbm.1) | copy-start | bytes 2654212
  19.1 1.2 %copy-start.4 = (bf16[27,128,128]{2,1,0:T(8,128)(2,1)S(1)}, bf16[27,128,128]{2,1,0:T(8,128)(2,1)}, u32[]{:S(2)}) copy-start(bf16[27,128,128]{2,1,0:T(8,128)(2,1)} %w_second_hbm.1) | copy-start | bytes 2654212
  20.2 0.9 %copy-start.5 = (bf16[7,64,128]{2,1,0:T(8,128)(2,1)S(1)}, bf16[7,64,128]{2,1,0:T(8,128)(2,1)}, u32[]{:S(2)}) copy-start(bf16[7,64,128]{2,1,0:T(8,128)(2,1)} %get-tuple-element.17.own) | copy-start | bytes 344068
  21.1 4.2 %copy-start.6 = (bf16[7,64,128]{2,1,0:T(8,128)(2,1)S(1)}, bf16[7,64,128]{2,1,0:T(8,128)(2,1)}, u32[]{:S(2)}) copy-start(bf16[7,64,128]{2,1,0:T(8,128)(2,1)} %get-tuple-element.17.own) | copy-start | bytes 344068
  42.9 32.5 %copy-start = (bf16[1,3,64,128]{3,2,1,0:T(8,128)(2,1)S(1)}, bf16[1,3,64,128]{3,2,1,0:T(8,128)(2,1)}, u32[]{:S(2)}) copy-start(bf16[1,3,64,128]{3,2,1,0:T(8,128)(2,1)} %features.3) | copy-start | bytes 147460
  42.9 32.5 %copy-start.1 = (bf16[1,3,64,128]{3,2,1,0:T(8,128)(2,1)S(1)}, bf16[1,3,64,128]{3,2,1,0:T(8,128)(2,1)}, u32[]{:S(2)}) copy-start(bf16[1,3,64,128]{3,2,1,0:T(8,128)(2,1)} %cotangent.3) | copy-start | bytes 147460
  42.9 32.5 %copy-start.2 = (s32[1,3]{1,0:T(1,128)S(1)}, s32[1,3]{1,0:T(1,128)}, u32[]{:S(2)}) copy-start(s32[1,3]{1,0:T(1,128)} %blocks.3) | copy-start | bytes 40
  64.5 22.4 %all-to-all-start.2 = ((bf16[24,14,128]{2,1,0:T(8,128)(2,1)}), bf16[24,14,128]{2,1,0:T(8,128)(2,1)S(1)}, u32[]{:S(2)}, u32[]{:S(2)}) async-start(bf16[24,14,128]{2,1,0:T(8,128)(2,1)} %bitcast.3), calls=%async_computation.2 | async-start | bytes 196608 | tf_op jit(solution)/shard_map/all_to_all | solution.py:406

commit v3 on v2

--- a/solution.py
+++ b/solution.py
@@ -343,6 +343,10 @@
     )
 
 
+def in_hbm(*arrays):
+    return [pltpu.with_memory_space_constraint(a, pltpu.HBM) for a in arrays]
+
+
 def shape(*dims, dtype=BF16):
     return jax.ShapeDtypeStruct(dims, dtype)
 
@@ -358,8 +362,8 @@
         [shape(1, 7, 32, C), shape(7, 64, C)],
         [pltpu.SMEM((1, SLOTS), jnp.int32), pltpu.SemaphoreType.DMA((5,))],
         1,
-        64,
-    )(blocks, features, cotangent)
+        40,
+    )(*in_hbm(blocks, features, cotangent))
     odd = range(1, 127, 2)
     partner = lax.ppermute(inner, "c", [(0, 1), (1, 0)])
     far = lax.ppermute(outer, TILE, [(t + 2, t) for t in range(0, 126, 2)] + [(t, t + 2) for t in range(1, 126, 2)])
@@ -378,7 +382,7 @@
         [pltpu.VMEM((3, 8, 10, 16, C), BF16), pltpu.SemaphoreType.DMA((2,))],
         2_000_000_000,
         40,
-    )(inner, partner, w_first, w_second)
+    )(inner, partner, *in_hbm(w_first, w_second))
     terms, hidden, first_grad = kernel_call(
         main_kernel,
         [VMEM] * 10,

time: 88.2 us -> 86 us (0.975)
  blocking collectives: 34.3 us -> 37.9 us
  local copies, waits for them, and re-layouts: 4.63 us -> 1.39 us
  starting transfers between devices: 26.5 us -> 24.4 us
    all_to_all x1, blocking collectives: 20.8 us -> 24.5 us  [on_device(): lax.all_to_all(along_x.transpose(1, 2, 0, 3), 'y', 0, 0, tiled=True)]
    unnamed x15 -> x7, local copies, waits for them, and re-layouts: 3.86 us -> 0.63 us
    all_to_all x1, starting transfers between devices: 10.9 us -> 8.79 us  [on_device(): lax.all_to_all(copies, ('zh', 'c', 'sa', 'sb'), 0, 0, tiled=True)]
  transfers between devices with their start and end apart: 4 -> 4, of which waited for: 1 -> 1; matrix products, arithmetic and copies ran while one was open for 0% -> 0% of each run, Pallas kernels for 8% -> 9%
where the time goes in v3:
time: 86 us; the launch traced here: 85.5 us
  blocking collectives  37.9 us (44%)
  starting transfers between devices  24.4 us (28%)
  Pallas kernels  12.6 us (15%)
  waiting for transfers between devices  8.15 us (9%)
  local copies, waits for them, and re-layouts  1.39 us (2%)
    all_to_all x1, blocking collectives, on_device(): lax.all_to_all(along_x.transpose(1, 2, 0, 3), 'y', 0, 0, tiled=True)  24.5 us
    all_to_all x1, blocking collectives, on_device(): lax.all_to_all(terms, ('x', 'sb'), 0, 0, tiled=True)  13.4 us
    ppermute x1, starting transfers between devices, on_device(): partner = lax.ppermute(inner, 'c', [(0, 1), (1, 0)])  12.4 us
    all_to_all x1, starting transfers between devices, on_device(): lax.all_to_all(copies, ('zh', 'c', 'sa', 'sb'), 0, 0, tiled=True)  8.79 us
    all_to_all x1, waiting for transfers between devices, on_device(): lax.all_to_all(copies, ('zh', 'c', 'sa', 'sb'), 0, 0, tiled=True)  8.14 us
    pallas_call x1, Pallas kernels, on_device(): kernel_call(chip_kernel, [VMEM, VMEM, HBM, HBM], [shape(27, C, C), shape(...  4.26 us
    pallas_call x1, Pallas kernels, on_device(): kernel_call(main_kernel, [VMEM] * 10, [shape(4, 2, 14, 32, C), shape(10,...  4.06 us
    pallas_call x1, Pallas kernels, on_device(): kernel_call(output_kernel, [SMEM] + [VMEM] * 6, [shape(1, SLOTS, 64, C)]...  3.34 us
  transfers between devices with their start and end apart: 4, of which 1 were waited for; matrix products, arithmetic and copies ran while one was open for 0% of the time, Pallas kernels for 9%

profile of v3, /device:TPU:1, one launch (start us, length us, event | category | flops | bytes accessed | tf_op | source)
XLA Modules:
  0.0 85.5 jit_solution(6161539128207570737)
XLA Ops:
  0.6 0.9 %shard_map.84 = (bf16[1,7,32,128]{3,2,1,0:T(8,128)(2,1)S(1)}, bf16[7,64,128]{2,1,0:T(8,128)(2,1)S(1)}) custom-call(s32[1,3]{1,0:T(1,128)} %blocks.3, bf16[1,3,64,128]{3,2,1,0:T(8,128)(2,1)} %features.3, bf16[1,3,64,128]{3,2,1,0:T(8,128)(2,1)} %cotangent.3), custom_call_target="tpu_custom_call" | custom-call | flops 1 | bytes 4000000 | tf_op jit(solution)/shard_map/pallas_call | solution.py:359
  1.6 12.4 %collective-permute-start = (bf16[7,64,128]{2,1,0:T(8,128)(2,1)S(1)}, bf16[7,64,128]{2,1,0:T(8,128)(2,1)S(1)}, u32[]{:S(2)}, u32[]{:S(2)}) collective-permute-start(bf16[7,64,128]{2,1,0:T(8,128)(2,1)S(1)} %get-tuple-element.17.own), channel_id=1, source_target_pairs={{0,6},{6,0},{1,7},{7,1},{2,8},{8,2},{3,9},{9,3},{4,10},{10,4},{5,1... | collective-permute-start | bytes 344072 | tf_op jit(solution)/shard_map/ppermute | solution.py:368
  14.0 1.9 %collective-permute-start.2 = (bf16[1,7,32,128]{3,2,1,0:T(8,128)(2,1)S(1)}, bf16[1,7,32,128]{3,2,1,0:T(8,128)(2,1)S(1)}, u32[]{:S(2)}, u32[]{:S(2)}) collective-permute-start(bf16[1,7,32,128]{3,2,1,0:T(8,128)(2,1)S(1)} %get-tuple-element.18), channel_id=1, source_target_pairs={{6,12},{18,24},{30,36},{42,48},{54,60},{66,72},{78,84},{90,96},{10... | collective-permute-start | bytes 172040 | tf_op jit(solution)/shard_map/ppermute | solution.py:370
  15.9 1.3 %collective-permute-start.1 = (bf16[1,7,32,128]{3,2,1,0:T(8,128)(2,1)S(1)}, bf16[1,7,32,128]{3,2,1,0:T(8,128)(2,1)S(1)}, u32[]{:S(2)}, u32[]{:S(2)}) collective-permute-start(bf16[1,7,32,128]{3,2,1,0:T(8,128)(2,1)S(1)} %get-tuple-element.18), channel_id=1, source_target_pairs={{12,0},{24,12},{36,24},{48,36},{60,48},{72,60},{84,72},{96,84},{10... | collective-permute-start | bytes 172040 | tf_op jit(solution)/shard_map/ppermute | solution.py:369
  17.2 0.0 collective-permute-done.partner
  17.2 4.3 %shard_map.85 = (bf16[27,128,128]{2,1,0:T(8,128)(2,1)S(1)}, bf16[27,128,128]{2,1,0:T(8,128)(2,1)S(1)}, bf16[3,8,10,16,128]{4,3,2,1,0:T(8,128)(2,1)S(1)}, bf16[12...) custom-call(bf16[7,64,128]{2,1,0:T(8,128)(2,1)S(1)} %get-tuple-element.17.own, ...), custom_call_target="tpu_custom_call" | custom-call | flops 2000000000 | bytes 4000000 | tf_op jit(solution)/shard_map/pallas_call | solution.py:371
  21.5 0.0 collective-permute-done.2.near
  21.5 0.0 collective-permute-done.1.far
  21.5 4.1 %shard_map.86 = (bf16[4,2,14,32,128]{4,3,2,1,0:T(8,128)(2,1)S(1)}, bf16[10,8,16,128]{3,2,1,0:T(8,128)(2,1)S(1)}, bf16[10,8,16,128]{3,2,1,0:T(8,128)(2,1)S(1)}) custom-call(bf16[7,64,128]{2,1,0:T(8,128)(2,1)S(1)} %get-tuple-element.17.own, bf16[7,64,128]{2,1,0:T(8,128)(2,1)S(1)} %collective-permute-done.partner, ...), custom_call_target="tpu_custom_call" | custom-call | flops 2000000000 | bytes 4000000 | tf_op jit(solution)/shard_map/pallas_call | solution.py:386
  25.6 13.4 %all_to_all.15 = bf16[8,14,32,128]{3,2,1,0:T(8,128)(2,1)S(1)} all-to-all(bf16[8,14,32,128]{3,2,1,0:T(8,128)(2,1)S(1)} %bitcast.12), channel_id=1, replica_groups=mesh['zh'=2,'y'=8,'x'=4,'c'=2,'sa'=3,'sb'=2] {'x','sb'}, dimensions={0} | all-to-all | bytes 1835008 | tf_op jit(solution)/shard_map/all_to_all | solution.py:407
  39.0 0.1 convert_reduce_fusion
  39.2 0.0 copy-start
  39.2 0.0 copy-start.1
  39.2 0.0 copy-start.2
  39.3 24.5 %all_to_all.16 = f32[8,4,14,128]{3,1,2,0:T(4,128)S(1)} all-to-all(f32[8,4,14,128]{3,1,2,0:T(4,128)S(1)} %copy.28), channel_id=1, replica_groups=mesh['zh'=2,'y'=8,'x'=4,'c'=2,'sa'=3,'sb'=2] {'y'}, dimensions={0} | all-to-all | bytes 458752 | tf_op jit(solution)/shard_map/all_to_all | solution.py:408
  63.8 0.6 broadcast_in_dim.2
  64.4 8.8 %all-to-all-start.2 = ((bf16[24,14,128]{2,1,0:T(8,128)(2,1)}), bf16[24,14,128]{2,1,0:T(8,128)(2,1)S(1)}, u32[]{:S(2)}, u32[]{:S(2)}) async-start(bf16[24,14,128]{2,1,0:T(8,128)(2,1)} %bitcast.3), calls=%async_computation.2 | async-start | bytes 196608 | tf_op jit(solution)/shard_map/all_to_all | solution.py:410
  73.2 0.0 copy-done
  73.2 0.0 copy-done.1
  73.3 0.0 copy-done.2
  73.3 3.3 %shard_map.87 = (bf16[1,3,64,128]{3,2,1,0:T(8,128)(2,1)}, bf16[1,3,64,128]{3,2,1,0:T(8,128)(2,1)}) custom-call(s32[1,3]{1,0:T(1,128)S(1)} %copy-done.2, bf16[1,3,64,128]{3,2,1,0:T(8,128)(2,1)S(1)} %copy-done, bf16[1,3,64,128]{3,2,1,0:T(8,128)(2,1)S(1)} %copy-done.1, bf16[10,8,16,128]{3,2,1,0:T(8,128)(2,1)S(1)} %get-tuple-element.25.hidden, ...), custom_call_target="tpu_custom_call" | custom-call | flops 1400000000 | bytes 4000000 | tf_op jit(solution)/shard_map/pallas_call | solution.py:399
  76.6 8.1 %all-to-all-done.2 = bf16[24,14,128]{2,1,0:T(8,128)(2,1)S(1)} async-done(((bf16[24,14,128]{2,1,0:T(8,128)(2,1)}), bf16[24,14,128]{2,1,0:T(8,128)(2,1)S(1)}, u32[]{:S(2)}, u32[]{:S(2)}) %all-to-all-start.2) | async-done | bytes 86048 | tf_op jit(solution)/shard_map/all_to_all | solution.py:410
  84.8 0.1 convert_reduce_fusion.1
  84.9 0.6 copy_bitcast_fusion
  (6 shorter events, 0.2 us)
Async XLA Ops:
  1.6 15.7 %collective-permute-start = (bf16[7,64,128]{2,1,0:T(8,128)(2,1)S(1)}, bf16[7,64,128]{2,1,0:T(8,128)(2,1)S(1)}, u32[]{:S(2)}, u32[]{:S(2)}) collective-permute-start(bf16[7,64,128]{2,1,0:T(8,128)(2,1)S(1)} %get-tuple-element.17.own), channel_id=1, source_target_pairs={{0,6},{6,0},{1,7},{7,1},{2,8},{8,2},{3,9},{9,3},{4,10},{10,4},{5,1... | collective-permute-start | bytes 344072 | tf_op jit(solution)/shard_map/ppermute | solution.py:368
  14.0 7.5 %collective-permute-start.2 = (bf16[1,7,32,128]{3,2,1,0:T(8,128)(2,1)S(1)}, bf16[1,7,32,128]{3,2,1,0:T(8,128)(2,1)S(1)}, u32[]{:S(2)}, u32[]{:S(2)}) collective-permute-start(bf16[1,7,32,128]{3,2,1,0:T(8,128)(2,1)S(1)} %get-tuple-element.18), channel_id=1, source_target_pairs={{6,12},{18,24},{30,36},{42,48},{54,60},{66,72},{78,84},{90,96},{10... | collective-permute-start | bytes 172040 | tf_op jit(solution)/shard_map/ppermute | solution.py:370
  15.9 5.6 %collective-permute-start.1 = (bf16[1,7,32,128]{3,2,1,0:T(8,128)(2,1)S(1)}, bf16[1,7,32,128]{3,2,1,0:T(8,128)(2,1)S(1)}, u32[]{:S(2)}, u32[]{:S(2)}) collective-permute-start(bf16[1,7,32,128]{3,2,1,0:T(8,128)(2,1)S(1)} %get-tuple-element.18), channel_id=1, source_target_pairs={{12,0},{24,12},{36,24},{48,36},{60,48},{72,60},{84,72},{96,84},{10... | collective-permute-start | bytes 172040 | tf_op jit(solution)/shard_map/ppermute | solution.py:369
  39.2 34.1 %copy-start = (bf16[1,3,64,128]{3,2,1,0:T(8,128)(2,1)S(1)}, bf16[1,3,64,128]{3,2,1,0:T(8,128)(2,1)}, u32[]{:S(2)}) copy-start(bf16[1,3,64,128]{3,2,1,0:T(8,128)(2,1)} %features.3) | copy-start | bytes 147460
  39.2 34.1 %copy-start.1 = (bf16[1,3,64,128]{3,2,1,0:T(8,128)(2,1)S(1)}, bf16[1,3,64,128]{3,2,1,0:T(8,128)(2,1)}, u32[]{:S(2)}) copy-start(bf16[1,3,64,128]{3,2,1,0:T(8,128)(2,1)} %cotangent.3) | copy-start | bytes 147460
  39.2 34.1 %copy-start.2 = (s32[1,3]{1,0:T(1,128)S(1)}, s32[1,3]{1,0:T(1,128)}, u32[]{:S(2)}) copy-start(s32[1,3]{1,0:T(1,128)} %blocks.3) | copy-start | bytes 40
  64.4 20.3 %all-to-all-start.2 = ((bf16[24,14,128]{2,1,0:T(8,128)(2,1)}), bf16[24,14,128]{2,1,0:T(8,128)(2,1)S(1)}, u32[]{:S(2)}, u32[]{:S(2)}) async-start(bf16[24,14,128]{2,1,0:T(8,128)(2,1)} %bitcast.3), calls=%async_computation.2 | async-start | bytes 196608 | tf_op jit(solution)/shard_map/all_to_all | solution.py:410

commit v4 on v3

--- a/solution.py
+++ b/solution.py
@@ -15,8 +15,8 @@
 BF16 = jnp.bfloat16
 
 
-def fetch(pairs, sems):
-    copies = [pltpu.make_async_copy(src, dst, sems.at[k]) for k, (src, dst) in enumerate(pairs)]
+def fetch(pairs, sems, first=0):
+    copies = [pltpu.make_async_copy(src, dst, sems.at[first + k]) for k, (src, dst) in enumerate(pairs)]
     for copy in copies:
         copy.start()
     return copies
@@ -122,37 +122,47 @@
         out[c, :, 9] = jnp.zeros((layers, 16, C), BF16)
 
 
-def taps(shifted, weights, layers):
-    lhs = jnp.concatenate(
-        [shifted[c, :, b : b + 8].reshape(layers * 128, C) for b in range(3) for c in range(3)], axis=1
-    )
-    rhs = jnp.concatenate([weights[9 * a : 9 * a + 9].reshape(9 * C, C) for a in range(3)], axis=1)
-    return jnp.dot(lhs, rhs, preferred_element_type=F32).reshape(layers, 128, 3 * C)
-
-
-def taps_back(shifted, weights, layers):
-    lhs = jnp.concatenate(
-        [shifted[2 - c, :, 2 - b : 10 - b].reshape(layers * 128, C) for b in range(3) for c in range(3)], axis=1
-    )
-    rhs = jnp.concatenate(
-        [jnp.concatenate([weights[9 * (2 - a) + k] for k in range(9)], axis=1) for a in range(3)], axis=0
-    )
-    out = lax.dot_general(lhs, rhs, (((1,), (1,)), ((), ())), preferred_element_type=F32)
-    return out.reshape(layers, 128, 3 * C)
-
-
-def thirds(out):
-    return out[:, :, 0:C], out[:, :, C : 2 * C], out[:, :, 2 * C : 3 * C]
+def patches(shifted, first, layers, back):
+    rows = pl.ds(first, layers)
+    return [
+        (shifted[2 - c, rows, 2 - b : 10 - b] if back else shifted[c, rows, b : b + 8]).reshape(layers * 128, C)
+        for b in range(3)
+        for c in range(3)
+    ]
+
+
+def matrices(weights, k, back):
+    return [weights[9 * (2 - k if back else k) + j] for j in range(9)]
+
+
+def product(pieces, columns, layers, back):
+    lhs = jnp.concatenate(pieces, axis=1)
+    rhs = jnp.concatenate([jnp.concatenate(col, axis=1 if back else 0) for col in columns], axis=0 if back else 1)
+    out = lax.dot_general(lhs, rhs, (((1,), (1 if back else 0,)), ((), ())), preferred_element_type=F32)
+    out = out.reshape(layers, 128, len(columns) * C)
+    return [out[:, :, n * C : (n + 1) * C] for n in range(len(columns))]
+
+
+def taps(shifted, weights, layers, back=False):
+    pieces = patches(shifted, 0, layers, back)
+    after, same = product(pieces, [matrices(weights, 0, back), matrices(weights, 1, back)], layers, back)
+    last = matrices(weights, 2, back)
+    none = jnp.zeros((C, C), BF16)
+    before, aside = product(pieces[:6], [last[:6], [none] * 3 + last[6:]], layers, back)
+    aside = aside.reshape(layers, 8, 16, C)
+    edge = jnp.zeros((layers, 1, 16, C), F32)
+    moved = [edge, aside[:, :7]] if back else [aside[:, 1:], edge]
+    return after, same, before + jnp.concatenate(moved, axis=1).reshape(layers, 128, C)
 
 
 def inside(out, layers):
-    after, same, before = thirds(out)
+    after, same, before = out
     n = layers - 2
     return after[0:n] + same[1 : n + 1] + before[2 : n + 2]
 
 
 def spread(out):
-    after, same, before = thirds(out)
+    after, same, before = out
     none = jnp.zeros((1, 128, C), F32)
     return (
         jnp.concatenate([none, none, after], axis=0)
@@ -161,15 +171,20 @@
     )
 
 
-def completed(part, out):
-    after, same, before = thirds(out)
+def completed(part, shifted, weights, back=False):
+    after, left = product(
+        patches(shifted, 0, 2, back), [matrices(weights, 0, back), matrices(weights, 1, back)], 2, back
+    )
+    right, before = product(
+        patches(shifted, 2, 2, back), [matrices(weights, 1, back), matrices(weights, 2, back)], 2, back
+    )
     return jnp.concatenate(
         [
-            part[0:1] + after[0:1] + same[1:2],
+            part[0:1] + after[0:1] + left[1:2],
             part[1:2] + after[1:2],
             part[2:8],
-            part[8:9] + before[2:3],
-            part[9:10] + same[2:3] + before[3:4],
+            part[8:9] + before[0:1],
+            part[9:10] + right[0:1] + before[1:2],
         ],
         axis=0,
     )
@@ -221,7 +236,8 @@
     w_first, w_second, field_z, upstream_pad, act_part, grad_part,
     upstream_z, sems,
 ):
-    copies = fetch([(w_first_hbm, w_first), (w_second_hbm, w_second)], sems)
+    thirds = [pl.ds(9 * k, 9) for k in range(3)]
+    one = fetch([(w_first_hbm.at[k], w_first.at[k]) for k in thirds], sems, 0)
     even = lax.axis_index("c") == 0
     masks = [block_masks(ids) for ids in chip_ids(own, partner, even)]
 
@@ -235,13 +251,16 @@
         return jnp.concatenate(parts, axis=0)
 
     store_shifted(field_z, field(0), 8)
+    two = fetch([(w_second_hbm.at[k], w_second.at[k]) for k in thirds], sems, 3)
     upstream = field(1)
     store_shifted(upstream_z, upstream, 8)
     pad_store(upstream_pad, upstream)
-    copies[0].wait()
+    for copy in one:
+        copy.wait()
     act_part[...] = spread(taps(field_z, w_first, 8))
-    copies[1].wait()
-    grad_part[...] = spread(taps_back(upstream_z, w_second, 8))
+    for copy in two:
+        copy.wait()
+    grad_part[...] = spread(taps(upstream_z, w_second, 8, True))
 
 
 def main_kernel(
@@ -266,7 +285,7 @@
 
     store_shifted(outer_z, field(0), 4)
     store_shifted(outer_up_z, field(1), 4)
-    first_act = completed(act_part[...], taps(outer_z, w_first, 4)).reshape(10, 8, 16, C)
+    first_act = completed(act_part[...], outer_z, w_first).reshape(10, 8, 16, C)
     live = jnp.concatenate(
         [
             live_tiles(left)[None],
@@ -280,7 +299,7 @@
     hidden = live * (first_act * gate)
     hidden_out[...] = hidden.astype(BF16)
     slope = live * (gate * (1.0 + first_act * (1.0 - gate)))
-    hidden_grad = completed(grad_part[...], taps_back(outer_up_z, w_second, 4)).reshape(10, 8, 16, C)
+    hidden_grad = completed(grad_part[...], outer_up_z, w_second, True).reshape(10, 8, 16, C)
     grad_out[...] = (hidden_grad * slope).astype(BF16)
 
     @pl.when(even)
@@ -319,11 +338,31 @@
     store_shifted(hidden_z, hidden[mine].astype(F32), 6)
     store_shifted(grad_z, first_grad[mine].astype(F32), 6)
     second_act = from_slab(inside(taps(hidden_z, w_second, 6), 6).reshape(4, 8, 16, C), own, 4)
-    back = from_slab(inside(taps_back(grad_z, w_first, 6), 6).reshape(4, 8, 16, C), own, 4)
+    back = from_slab(inside(taps(grad_z, w_first, 6, True), 6).reshape(4, 8, 16, C), own, 4)
     for j in range(SLOTS):
         live = jnp.where(blocks[0, j] < BY * BZ, 1.0, 0.0)
         block_out[0, j] = (live * (features[0, j].astype(F32) + second_act[j])).astype(BF16)
         input_grad[0, j] = (live * (cotangent[0, j].astype(F32) + back[j])).astype(BF16)
+
+
+def repeat_kernel(pieces, out):
+    total = pieces[0]
+    for k in range(1, 8):
+        total = total + pieces[k]
+    total = total.astype(BF16)
+    for n in range(4):
+        for k in range(6):
+            out[6 * n + k] = total[n]
+
+
+def last_kernel(pieces, first, second):
+    for c, out in enumerate((first, second)):
+        for sb, rows in enumerate((14, 13)):
+            parts = [pieces[zh * 12 + c * 6 + sa * 2 + sb].astype(F32) for zh in range(2) for sa in range(3)]
+            total = parts[0]
+            for part in parts[1:]:
+                total = total + part
+            out[14 * sb : 14 * sb + rows] = total[0:rows]
 
 
 VMEM = pl.BlockSpec(memory_space=pltpu.VMEM)
@@ -379,7 +418,7 @@
             shape(10, 128, C, dtype=F32),
             shape(10, 128, C, dtype=F32),
         ],
-        [pltpu.VMEM((3, 8, 10, 16, C), BF16), pltpu.SemaphoreType.DMA((2,))],
+        [pltpu.VMEM((3, 8, 10, 16, C), BF16), pltpu.SemaphoreType.DMA((6,))],
         2_000_000_000,
         40,
     )(inner, partner, *in_hbm(w_first, w_second))
@@ -405,11 +444,11 @@
     )(blocks, features, cotangent, hidden, first_grad, w_first, w_second)
     terms = terms.reshape(8, 14, 32, C)
     along_x = folded(lax.all_to_all(terms, ("x", "sb"), 0, 0, tiled=True)).reshape(14, 8, 4, C)
-    along_y = folded(lax.all_to_all(along_x.transpose(1, 2, 0, 3), "y", 0, 0, tiled=True)).astype(BF16)
-    copies = jnp.broadcast_to(along_y[:, None], (4, 6, 14, C)).reshape(24, 14, C)
-    pieces = lax.all_to_all(copies, ("zh", "c", "sa", "sb"), 0, 0, tiled=True).reshape(2, 2, 3, 2, 14, C)
-    total = pieces.astype(F32).sum(axis=(0, 2)).reshape(2, 28, C)
-    return block_out, input_grad, total[0, :27], total[1, :27]
+    along_y = lax.all_to_all(along_x.transpose(1, 2, 0, 3), "y", 0, 0, tiled=True)
+    copies = kernel_call(repeat_kernel, [VMEM], [shape(24, 14, C)], [], 1, 40)(along_y)[0]
+    pieces = lax.all_to_all(copies, ("zh", "c", "sa", "sb"), 0, 0, tiled=True)
+    first_total, second_total = kernel_call(last_kernel, [VMEM], [shape(27, C, dtype=F32)] * 2, [], 1, 40)(pieces)
+    return block_out, input_grad, first_total, second_total
 
 
 def solution(mesh):

time: 86 us -> 85 us (0.988)
  local copies, waits for them, and re-layouts: 1.39 us -> 0.09 us
    pallas_call x0 -> x2, Pallas kernels: none -> 1.28 us  [the longest x1 0.66 us: on_device(): kernel_call(repeat_kernel, [VMEM], [shape(24, 14, C)], [], 1, 40)(along_y)]
where the time goes in v4:
time: 85 us; the launch traced here: 84.6 us
  blocking collectives  38 us (45%)
  starting transfers between devices  24.3 us (29%)
  Pallas kernels  12.8 us (15%)
  waiting for transfers between devices  8.5 us (10%)
    all_to_all x1, blocking collectives, on_device(): lax.all_to_all(along_x.transpose(1, 2, 0, 3), 'y', 0, 0, tiled=True)  24.6 us
    all_to_all x1, blocking collectives, on_device(): lax.all_to_all(terms, ('x', 'sb'), 0, 0, tiled=True)  13.4 us
    ppermute x1, starting transfers between devices, on_device(): partner = lax.ppermute(inner, 'c', [(0, 1), (1, 0)])  12.4 us
    all_to_all x1, starting transfers between devices, on_device(): pieces = lax.all_to_all(copies, ('zh', 'c', 'sa', 'sb'), 0, 0, tiled=True)  8.7 us
    all_to_all x1, waiting for transfers between devices, on_device(): pieces = lax.all_to_all(copies, ('zh', 'c', 'sa', 'sb'), 0, 0, tiled=True)  8.49 us
    pallas_call x1, Pallas kernels, on_device(): kernel_call(chip_kernel, [VMEM, VMEM, HBM, HBM], [shape(27, C, C), shape(...  4.27 us
    pallas_call x1, Pallas kernels, on_device(): kernel_call(main_kernel, [VMEM] * 10, [shape(4, 2, 14, 32, C), shape(10,...  3.3 us
    pallas_call x1, Pallas kernels, on_device(): kernel_call(output_kernel, [SMEM] + [VMEM] * 6, [shape(1, SLOTS, 64, C)]...  2.99 us
  transfers between devices with their start and end apart: 4, of which 1 were waited for; matrix products, arithmetic and copies ran while one was open for 0% of the time, Pallas kernels for 9%

profile of v4, /device:TPU:1, one launch (start us, length us, event | category | flops | bytes accessed | tf_op | source)
XLA Modules:
  0.0 84.6 jit_solution(7528242985956461691)
XLA Ops:
  0.6 0.9 %shard_map.84 = (bf16[1,7,32,128]{3,2,1,0:T(8,128)(2,1)S(1)}, bf16[7,64,128]{2,1,0:T(8,128)(2,1)S(1)}) custom-call(s32[1,3]{1,0:T(1,128)} %blocks.3, bf16[1,3,64,128]{3,2,1,0:T(8,128)(2,1)} %features.3, bf16[1,3,64,128]{3,2,1,0:T(8,128)(2,1)} %cotangent.3), custom_call_target="tpu_custom_call" | custom-call | flops 1 | bytes 4000000 | tf_op jit(solution)/shard_map/pallas_call | solution.py:398
  1.6 12.4 %collective-permute-start = (bf16[7,64,128]{2,1,0:T(8,128)(2,1)S(1)}, bf16[7,64,128]{2,1,0:T(8,128)(2,1)S(1)}, u32[]{:S(2)}, u32[]{:S(2)}) collective-permute-start(bf16[7,64,128]{2,1,0:T(8,128)(2,1)S(1)} %get-tuple-element.19.own), channel_id=1, source_target_pairs={{0,6},{6,0},{1,7},{7,1},{2,8},{8,2},{3,9},{9,3},{4,10},{10,4},{5,1... | collective-permute-start | bytes 344072 | tf_op jit(solution)/shard_map/ppermute | solution.py:407
  14.0 1.9 %collective-permute-start.2 = (bf16[1,7,32,128]{3,2,1,0:T(8,128)(2,1)S(1)}, bf16[1,7,32,128]{3,2,1,0:T(8,128)(2,1)S(1)}, u32[]{:S(2)}, u32[]{:S(2)}) collective-permute-start(bf16[1,7,32,128]{3,2,1,0:T(8,128)(2,1)S(1)} %get-tuple-element.20), channel_id=1, source_target_pairs={{6,12},{18,24},{30,36},{42,48},{54,60},{66,72},{78,84},{90,96},{10... | collective-permute-start | bytes 172040 | tf_op jit(solution)/shard_map/ppermute | solution.py:409
  15.9 1.3 %collective-permute-start.1 = (bf16[1,7,32,128]{3,2,1,0:T(8,128)(2,1)S(1)}, bf16[1,7,32,128]{3,2,1,0:T(8,128)(2,1)S(1)}, u32[]{:S(2)}, u32[]{:S(2)}) collective-permute-start(bf16[1,7,32,128]{3,2,1,0:T(8,128)(2,1)S(1)} %get-tuple-element.20), channel_id=1, source_target_pairs={{12,0},{24,12},{36,24},{48,36},{60,48},{72,60},{84,72},{96,84},{10... | collective-permute-start | bytes 172040 | tf_op jit(solution)/shard_map/ppermute | solution.py:408
  17.2 0.0 collective-permute-done.partner
  17.2 4.3 %shard_map.85 = (bf16[27,128,128]{2,1,0:T(8,128)(2,1)S(1)}, bf16[27,128,128]{2,1,0:T(8,128)(2,1)S(1)}, bf16[3,8,10,16,128]{4,3,2,1,0:T(8,128)(2,1)S(1)}, bf16[12...) custom-call(bf16[7,64,128]{2,1,0:T(8,128)(2,1)S(1)} %get-tuple-element.19.own, ...), custom_call_target="tpu_custom_call" | custom-call | flops 2000000000 | bytes 4000000 | tf_op jit(solution)/shard_map/pallas_call | solution.py:410
  21.5 0.0 collective-permute-done.2.near
  21.5 0.0 collective-permute-done.1.far
  21.5 3.3 %shard_map.86 = (bf16[4,2,14,32,128]{4,3,2,1,0:T(8,128)(2,1)S(1)}, bf16[10,8,16,128]{3,2,1,0:T(8,128)(2,1)S(1)}, bf16[10,8,16,128]{3,2,1,0:T(8,128)(2,1)S(1)}) custom-call(bf16[7,64,128]{2,1,0:T(8,128)(2,1)S(1)} %get-tuple-element.19.own, bf16[7,64,128]{2,1,0:T(8,128)(2,1)S(1)} %collective-permute-done.partner, ...), custom_call_target="tpu_custom_call" | custom-call | flops 2000000000 | bytes 4000000 | tf_op jit(solution)/shard_map/pallas_call | solution.py:425
  24.9 13.4 %all_to_all.15 = bf16[8,14,32,128]{3,2,1,0:T(8,128)(2,1)S(1)} all-to-all(bf16[8,14,32,128]{3,2,1,0:T(8,128)(2,1)S(1)} %bitcast.5), channel_id=1, replica_groups=mesh['zh'=2,'y'=8,'x'=4,'c'=2,'sa'=3,'sb'=2] {'x','sb'}, dimensions={0} | all-to-all | bytes 1835008 | tf_op jit(solution)/shard_map/all_to_all | solution.py:446
  38.3 0.1 convert_reduce_fusion
  38.4 0.0 copy-start
  38.4 0.0 copy-start.1
  38.4 0.0 copy-start.2
  38.5 24.6 %all_to_all.16 = f32[8,4,14,128]{3,1,2,0:T(4,128)S(1)} all-to-all(f32[8,4,14,128]{3,1,2,0:T(4,128)S(1)} %bitcast.6), channel_id=1, replica_groups=mesh['zh'=2,'y'=8,'x'=4,'c'=2,'sa'=3,'sb'=2] {'y'}, dimensions={0} | all-to-all | bytes 458752 | tf_op jit(solution)/shard_map/all_to_all | solution.py:447
  63.1 0.7 shard_map.88
  63.8 8.7 %all-to-all-start.2 = ((bf16[24,14,128]{2,1,0:T(8,128)(2,1)}), bf16[24,14,128]{2,1,0:T(8,128)(2,1)S(1)}, u32[]{:S(2)}, u32[]{:S(2)}) async-start(bf16[24,14,128]{2,1,0:T(8,128)(2,1)} %shard_map.88), calls=%async_computation.2 | async-start | bytes 196608 | tf_op jit(solution)/shard_map/all_to_all | solution.py:449
  72.5 0.0 copy-done
  72.5 0.0 copy-done.1
  72.5 0.0 copy-done.2
  72.5 3.0 %shard_map.87 = (bf16[1,3,64,128]{3,2,1,0:T(8,128)(2,1)}, bf16[1,3,64,128]{3,2,1,0:T(8,128)(2,1)}) custom-call(s32[1,3]{1,0:T(1,128)S(1)} %copy-done.2, bf16[1,3,64,128]{3,2,1,0:T(8,128)(2,1)S(1)} %copy-done, bf16[1,3,64,128]{3,2,1,0:T(8,128)(2,1)S(1)} %copy-done.1, bf16[10,8,16,128]{3,2,1,0:T(8,128)(2,1)S(1)} %get-tuple-element.27.hidden, ...), custom_call_target="tpu_custom_call" | custom-call | flops 1400000000 | bytes 4000000 | tf_op jit(solution)/shard_map/pallas_call | solution.py:438
  75.5 8.5 %all-to-all-done.2.pieces = bf16[24,14,128]{2,1,0:T(8,128)(2,1)S(1)} async-done(((bf16[24,14,128]{2,1,0:T(8,128)(2,1)}), bf16[24,14,128]{2,1,0:T(8,128)(2,1)S(1)}, u32[]{:S(2)}, u32[]{:S(2)}) %all-to-all-start.2) | async-done | bytes 86048 | tf_op jit(solution)/shard_map/all_to_all | solution.py:449
  84.0 0.6 shard_map.89
  (2 shorter events, 0.1 us)
Async XLA Ops:
  1.6 15.7 %collective-permute-start = (bf16[7,64,128]{2,1,0:T(8,128)(2,1)S(1)}, bf16[7,64,128]{2,1,0:T(8,128)(2,1)S(1)}, u32[]{:S(2)}, u32[]{:S(2)}) collective-permute-start(bf16[7,64,128]{2,1,0:T(8,128)(2,1)S(1)} %get-tuple-element.19.own), channel_id=1, source_target_pairs={{0,6},{6,0},{1,7},{7,1},{2,8},{8,2},{3,9},{9,3},{4,10},{10,4},{5,1... | collective-permute-start | bytes 344072 | tf_op jit(solution)/shard_map/ppermute | solution.py:407
  14.0 7.5 %collective-permute-start.2 = (bf16[1,7,32,128]{3,2,1,0:T(8,128)(2,1)S(1)}, bf16[1,7,32,128]{3,2,1,0:T(8,128)(2,1)S(1)}, u32[]{:S(2)}, u32[]{:S(2)}) collective-permute-start(bf16[1,7,32,128]{3,2,1,0:T(8,128)(2,1)S(1)} %get-tuple-element.20), channel_id=1, source_target_pairs={{6,12},{18,24},{30,36},{42,48},{54,60},{66,72},{78,84},{90,96},{10... | collective-permute-start | bytes 172040 | tf_op jit(solution)/shard_map/ppermute | solution.py:409
  15.9 5.6 %collective-permute-start.1 = (bf16[1,7,32,128]{3,2,1,0:T(8,128)(2,1)S(1)}, bf16[1,7,32,128]{3,2,1,0:T(8,128)(2,1)S(1)}, u32[]{:S(2)}, u32[]{:S(2)}) collective-permute-start(bf16[1,7,32,128]{3,2,1,0:T(8,128)(2,1)S(1)} %get-tuple-element.20), channel_id=1, source_target_pairs={{12,0},{24,12},{36,24},{48,36},{60,48},{72,60},{84,72},{96,84},{10... | collective-permute-start | bytes 172040 | tf_op jit(solution)/shard_map/ppermute | solution.py:408
  38.4 34.1 %copy-start = (bf16[1,3,64,128]{3,2,1,0:T(8,128)(2,1)S(1)}, bf16[1,3,64,128]{3,2,1,0:T(8,128)(2,1)}, u32[]{:S(2)}) copy-start(bf16[1,3,64,128]{3,2,1,0:T(8,128)(2,1)} %features.3) | copy-start | bytes 147460
  38.4 34.1 %copy-start.1 = (bf16[1,3,64,128]{3,2,1,0:T(8,128)(2,1)S(1)}, bf16[1,3,64,128]{3,2,1,0:T(8,128)(2,1)}, u32[]{:S(2)}) copy-start(bf16[1,3,64,128]{3,2,1,0:T(8,128)(2,1)} %cotangent.3) | copy-start | bytes 147460
  38.4 34.1 %copy-start.2 = (s32[1,3]{1,0:T(1,128)S(1)}, s32[1,3]{1,0:T(1,128)}, u32[]{:S(2)}) copy-start(s32[1,3]{1,0:T(1,128)} %blocks.3) | copy-start | bytes 40
  63.8 20.2 %all-to-all-start.2 = ((bf16[24,14,128]{2,1,0:T(8,128)(2,1)}), bf16[24,14,128]{2,1,0:T(8,128)(2,1)S(1)}, u32[]{:S(2)}, u32[]{:S(2)}) async-start(bf16[24,14,128]{2,1,0:T(8,128)(2,1)} %shard_map.88), calls=%async_computation.2 | async-start | bytes 196608 | tf_op jit(solution)/shard_map/all_to_all | solution.py:449

commit v5 on v4

--- a/solution.py
+++ b/solution.py
@@ -9,7 +9,7 @@
 BZ = 4
 C = 128
 SLOTS = 3
-TILE = ("zh", "y", "x", "c")
+TILE = ("zh", "ya", "yb", "x", "c")
 SCENE = ("sa", "sb")
 F32 = jnp.float32
 BF16 = jnp.bfloat16
@@ -205,8 +205,8 @@
             for c in range(3):
                 piece = out[c * C : (c + 1) * C, (3 * a + b) * C : (3 * a + b + 1) * C]
                 half, tap = divmod(9 * a + 3 * b + c, 14)
-                terms[:, half, tap] = piece.astype(BF16).reshape(4, 32, C)
-    terms[:, 1, 13] = jnp.zeros((4, 32, C), BF16)
+                terms[:, half, tap] = piece.astype(BF16).reshape(8, 16, C)
+    terms[:, 1, 13] = jnp.zeros((8, 16, C), BF16)
 
 
 def pad_store(out, slab):
@@ -318,7 +318,8 @@
 
     r = lax.broadcasted_iota(jnp.int32, (C, C), 0)
     i = lax.broadcasted_iota(jnp.int32, (C, C), 1)
-    wanted = (((r // 2) % 2 * 8 + (r // 4) % 8) * 4 + r // 32) * 2 + r % 2
+    y = (r // 4) % 4 * 2 + r // 64
+    wanted = (((r // 2) % 2 * 8 + y) * 4 + (r // 16) % 4) * 2 + r % 2
     order = jnp.where(i == wanted, 1.0, 0.0).astype(BF16)
     weight_terms(
         order,
@@ -347,7 +348,7 @@
 
 def repeat_kernel(pieces, out):
     total = pieces[0]
-    for k in range(1, 8):
+    for k in range(1, 4):
         total = total + pieces[k]
     total = total.astype(BF16)
     for n in range(4):
@@ -425,7 +426,7 @@
     terms, hidden, first_grad = kernel_call(
         main_kernel,
         [VMEM] * 10,
-        [shape(4, 2, 14, 32, C), shape(10, 8, 16, C), shape(10, 8, 16, C)],
+        [shape(8, 2, 14, 16, C), shape(10, 8, 16, C), shape(10, 8, 16, C)],
         [
             pltpu.VMEM((3, 4, 10, 16, C), BF16),
             pltpu.VMEM((3, 4, 10, 16, C), BF16),
@@ -442,9 +443,9 @@
         [pltpu.VMEM((3, 6, 10, 16, C), BF16), pltpu.VMEM((3, 6, 10, 16, C), BF16)],
         1_400_000_000,
     )(blocks, features, cotangent, hidden, first_grad, w_first, w_second)
-    terms = terms.reshape(8, 14, 32, C)
-    along_x = folded(lax.all_to_all(terms, ("x", "sb"), 0, 0, tiled=True)).reshape(14, 8, 4, C)
-    along_y = lax.all_to_all(along_x.transpose(1, 2, 0, 3), "y", 0, 0, tiled=True)
+    terms = terms.reshape(16, 14, 16, C)
+    along_x = folded(lax.all_to_all(terms, ("yb", "x", "sb"), 0, 0, tiled=True)).reshape(14, 4, 4, C)
+    along_y = lax.all_to_all(along_x.transpose(1, 2, 0, 3), "ya", 0, 0, tiled=True)
     copies = kernel_call(repeat_kernel, [VMEM], [shape(24, 14, C)], [], 1, 40)(along_y)[0]
     pieces = lax.all_to_all(copies, ("zh", "c", "sa", "sb"), 0, 0, tiled=True)
     first_total, second_total = kernel_call(last_kernel, [VMEM], [shape(27, C, dtype=F32)] * 2, [], 1, 40)(pieces)
@@ -452,7 +453,7 @@
 
 
 def solution(mesh):
-    split = Mesh(mesh.devices.reshape(2, 8, 4, 2, 3, 2), TILE + SCENE)
+    split = Mesh(mesh.devices.reshape(2, 4, 2, 4, 2, 3, 2), TILE + SCENE)
     return jax.shard_map(
         on_device,
         mesh=split,

time: 85 us -> 83.7 us (0.985)
  blocking collectives: 38 us -> 35.7 us
  starting transfers between devices: 24.3 us -> 25.3 us
    all_to_all x2, blocking collectives: 38 us -> 35.7 us  [the longest x1 22.5 us: on_device(): lax.all_to_all(along_x.transpose(1, 2, 0, 3), 'ya', 0, 0, tiled=True)]
    all_to_all x1, starting transfers between devices: 8.7 us -> 9.69 us  [on_device(): pieces = lax.all_to_all(copies, ('zh', 'c', 'sa', 'sb'), 0, 0, tiled=True)]
where the time goes in v5:
time: 83.7 us; the launch traced here: 83.2 us
  blocking collectives  35.7 us (43%)
  starting transfers between devices  25.3 us (30%)
  Pallas kernels  12.8 us (15%)
  waiting for transfers between devices  8.5 us (10%)
    all_to_all x1, blocking collectives, on_device(): lax.all_to_all(along_x.transpose(1, 2, 0, 3), 'ya', 0, 0, tiled=True)  22.5 us
    all_to_all x1, blocking collectives, on_device(): lax.all_to_all(terms, ('yb', 'x', 'sb'), 0, 0, tiled=True)  13.1 us
    ppermute x1, starting transfers between devices, on_device(): partner = lax.ppermute(inner, 'c', [(0, 1), (1, 0)])  12.4 us
    all_to_all x1, starting transfers between devices, on_device(): pieces = lax.all_to_all(copies, ('zh', 'c', 'sa', 'sb'), 0, 0, tiled=True)  9.69 us
    all_to_all x1, waiting for transfers between devices, on_device(): pieces = lax.all_to_all(copies, ('zh', 'c', 'sa', 'sb'), 0, 0, tiled=True)  8.49 us
    pallas_call x1, Pallas kernels, on_device(): kernel_call(chip_kernel, [VMEM, VMEM, HBM, HBM], [shape(27, C, C), shape(...  4.27 us
    pallas_call x1, Pallas kernels, on_device(): kernel_call(main_kernel, [VMEM] * 10, [shape(8, 2, 14, 16, C), shape(10,...  3.31 us
    pallas_call x1, Pallas kernels, on_device(): kernel_call(output_kernel, [SMEM] + [VMEM] * 6, [shape(1, SLOTS, 64, C)]...  2.99 us
  transfers between devices with their start and end apart: 4, of which 1 were waited for; matrix products, arithmetic and copies ran while one was open for 0% of the time, Pallas kernels for 9%

profile of v5, /device:TPU:1, one launch (start us, length us, event | category | flops | bytes accessed | tf_op | source)
XLA Modules:
  0.0 83.2 jit_solution(15067214611015537989)
XLA Ops:
  0.6 0.9 %shard_map.84 = (bf16[1,7,32,128]{3,2,1,0:T(8,128)(2,1)S(1)}, bf16[7,64,128]{2,1,0:T(8,128)(2,1)S(1)}) custom-call(s32[1,3]{1,0:T(1,128)} %blocks.3, bf16[1,3,64,128]{3,2,1,0:T(8,128)(2,1)} %features.3, bf16[1,3,64,128]{3,2,1,0:T(8,128)(2,1)} %cotangent.3), custom_call_target="tpu_custom_call" | custom-call | flops 1 | bytes 4000000 | tf_op jit(solution)/shard_map/pallas_call | solution.py:399
  1.6 12.4 %collective-permute-start = (bf16[7,64,128]{2,1,0:T(8,128)(2,1)S(1)}, bf16[7,64,128]{2,1,0:T(8,128)(2,1)S(1)}, u32[]{:S(2)}, u32[]{:S(2)}) collective-permute-start(bf16[7,64,128]{2,1,0:T(8,128)(2,1)S(1)} %get-tuple-element.19.own), channel_id=1, source_target_pairs={{0,6},{6,0},{1,7},{7,1},{2,8},{8,2},{3,9},{9,3},{4,10},{10,4},{5,1... | collective-permute-start | bytes 344072 | tf_op jit(solution)/shard_map/ppermute | solution.py:408
  14.0 1.9 %collective-permute-start.2 = (bf16[1,7,32,128]{3,2,1,0:T(8,128)(2,1)S(1)}, bf16[1,7,32,128]{3,2,1,0:T(8,128)(2,1)S(1)}, u32[]{:S(2)}, u32[]{:S(2)}) collective-permute-start(bf16[1,7,32,128]{3,2,1,0:T(8,128)(2,1)S(1)} %get-tuple-element.20), channel_id=1, source_target_pairs={{6,12},{18,24},{30,36},{42,48},{54,60},{66,72},{78,84},{90,96},{10... | collective-permute-start | bytes 172040 | tf_op jit(solution)/shard_map/ppermute | solution.py:410
  15.9 1.3 %collective-permute-start.1 = (bf16[1,7,32,128]{3,2,1,0:T(8,128)(2,1)S(1)}, bf16[1,7,32,128]{3,2,1,0:T(8,128)(2,1)S(1)}, u32[]{:S(2)}, u32[]{:S(2)}) collective-permute-start(bf16[1,7,32,128]{3,2,1,0:T(8,128)(2,1)S(1)} %get-tuple-element.20), channel_id=1, source_target_pairs={{12,0},{24,12},{36,24},{48,36},{60,48},{72,60},{84,72},{96,84},{10... | collective-permute-start | bytes 172040 | tf_op jit(solution)/shard_map/ppermute | solution.py:409
  17.2 0.0 collective-permute-done.partner
  17.2 4.3 %shard_map.85 = (bf16[27,128,128]{2,1,0:T(8,128)(2,1)S(1)}, bf16[27,128,128]{2,1,0:T(8,128)(2,1)S(1)}, bf16[3,8,10,16,128]{4,3,2,1,0:T(8,128)(2,1)S(1)}, bf16[12...) custom-call(bf16[7,64,128]{2,1,0:T(8,128)(2,1)S(1)} %get-tuple-element.19.own, ...), custom_call_target="tpu_custom_call" | custom-call | flops 2000000000 | bytes 4000000 | tf_op jit(solution)/shard_map/pallas_call | solution.py:411
  21.5 0.0 collective-permute-done.2.near
  21.5 0.0 collective-permute-done.1.far
  21.5 3.3 %shard_map.86 = (bf16[8,2,14,16,128]{4,3,2,1,0:T(8,128)(2,1)S(1)}, bf16[10,8,16,128]{3,2,1,0:T(8,128)(2,1)S(1)}, bf16[10,8,16,128]{3,2,1,0:T(8,128)(2,1)S(1)}) custom-call(bf16[7,64,128]{2,1,0:T(8,128)(2,1)S(1)} %get-tuple-element.19.own, bf16[7,64,128]{2,1,0:T(8,128)(2,1)S(1)} %collective-permute-done.partner, ...), custom_call_target="tpu_custom_call" | custom-call | flops 2000000000 | bytes 4000000 | tf_op jit(solution)/shard_map/pallas_call | solution.py:426
  24.9 13.1 %all_to_all.15 = bf16[16,14,16,128]{3,2,1,0:T(8,128)(2,1)S(1)} all-to-all(bf16[16,14,16,128]{3,2,1,0:T(8,128)(2,1)S(1)} %bitcast.5), channel_id=1, replica_groups=mesh['zh'=2,'ya'=4,'yb'=2,'x'=4,'c'=2,'sa'=3,'sb'=2] {'yb','x','sb'}, dimensions={0} | all-to-all | bytes 1835008 | tf_op jit(solution)/shard_map/all_to_all | solution.py:447
  38.0 0.0 copy-start
  38.0 0.0 copy-start.1
  38.0 0.0 copy-start.2
  38.0 0.1 convert_reduce_fusion
  38.2 22.5 %all_to_all.16 = f32[4,4,14,128]{3,1,2,0:T(4,128)S(1)} all-to-all(f32[4,4,14,128]{3,1,2,0:T(4,128)S(1)} %bitcast.6), channel_id=1, replica_groups=mesh['zh'=2,'ya'=4,'yb'=2,'x'=4,'c'=2,'sa'=3,'sb'=2] {'ya'}, dimensions={0} | all-to-all | bytes 229376 | tf_op jit(solution)/shard_map/all_to_all | solution.py:448
  60.7 0.7 shard_map.88
  61.4 9.7 %all-to-all-start.2 = ((bf16[24,14,128]{2,1,0:T(8,128)(2,1)}), bf16[24,14,128]{2,1,0:T(8,128)(2,1)S(1)}, u32[]{:S(2)}, u32[]{:S(2)}) async-start(bf16[24,14,128]{2,1,0:T(8,128)(2,1)} %shard_map.88), calls=%async_computation.2 | async-start | bytes 196608 | tf_op jit(solution)/shard_map/all_to_all | solution.py:450
  71.1 0.0 copy-done
  71.1 0.0 copy-done.1
  71.1 0.0 copy-done.2
  71.1 3.0 %shard_map.87 = (bf16[1,3,64,128]{3,2,1,0:T(8,128)(2,1)}, bf16[1,3,64,128]{3,2,1,0:T(8,128)(2,1)}) custom-call(s32[1,3]{1,0:T(1,128)S(1)} %copy-done.2, bf16[1,3,64,128]{3,2,1,0:T(8,128)(2,1)S(1)} %copy-done, bf16[1,3,64,128]{3,2,1,0:T(8,128)(2,1)S(1)} %copy-done.1, bf16[10,8,16,128]{3,2,1,0:T(8,128)(2,1)S(1)} %get-tuple-element.27.hidden, ...), custom_call_target="tpu_custom_call" | custom-call | flops 1400000000 | bytes 4000000 | tf_op jit(solution)/shard_map/pallas_call | solution.py:439
  74.1 8.5 %all-to-all-done.2.pieces = bf16[24,14,128]{2,1,0:T(8,128)(2,1)S(1)} async-done(((bf16[24,14,128]{2,1,0:T(8,128)(2,1)}), bf16[24,14,128]{2,1,0:T(8,128)(2,1)S(1)}, u32[]{:S(2)}, u32[]{:S(2)}) %all-to-all-start.2) | async-done | bytes 86048 | tf_op jit(solution)/shard_map/all_to_all | solution.py:450
  82.6 0.6 shard_map.89
  (2 shorter events, 0.0 us)
Async XLA Ops:
  1.6 15.7 %collective-permute-start = (bf16[7,64,128]{2,1,0:T(8,128)(2,1)S(1)}, bf16[7,64,128]{2,1,0:T(8,128)(2,1)S(1)}, u32[]{:S(2)}, u32[]{:S(2)}) collective-permute-start(bf16[7,64,128]{2,1,0:T(8,128)(2,1)S(1)} %get-tuple-element.19.own), channel_id=1, source_target_pairs={{0,6},{6,0},{1,7},{7,1},{2,8},{8,2},{3,9},{9,3},{4,10},{10,4},{5,1... | collective-permute-start | bytes 344072 | tf_op jit(solution)/shard_map/ppermute | solution.py:408
  14.0 7.5 %collective-permute-start.2 = (bf16[1,7,32,128]{3,2,1,0:T(8,128)(2,1)S(1)}, bf16[1,7,32,128]{3,2,1,0:T(8,128)(2,1)S(1)}, u32[]{:S(2)}, u32[]{:S(2)}) collective-permute-start(bf16[1,7,32,128]{3,2,1,0:T(8,128)(2,1)S(1)} %get-tuple-element.20), channel_id=1, source_target_pairs={{6,12},{18,24},{30,36},{42,48},{54,60},{66,72},{78,84},{90,96},{10... | collective-permute-start | bytes 172040 | tf_op jit(solution)/shard_map/ppermute | solution.py:410
  15.9 5.6 %collective-permute-start.1 = (bf16[1,7,32,128]{3,2,1,0:T(8,128)(2,1)S(1)}, bf16[1,7,32,128]{3,2,1,0:T(8,128)(2,1)S(1)}, u32[]{:S(2)}, u32[]{:S(2)}) collective-permute-start(bf16[1,7,32,128]{3,2,1,0:T(8,128)(2,1)S(1)} %get-tuple-element.20), channel_id=1, source_target_pairs={{12,0},{24,12},{36,24},{48,36},{60,48},{72,60},{84,72},{96,84},{10... | collective-permute-start | bytes 172040 | tf_op jit(solution)/shard_map/ppermute | solution.py:409
  38.0 33.1 %copy-start = (bf16[1,3,64,128]{3,2,1,0:T(8,128)(2,1)S(1)}, bf16[1,3,64,128]{3,2,1,0:T(8,128)(2,1)}, u32[]{:S(2)}) copy-start(bf16[1,3,64,128]{3,2,1,0:T(8,128)(2,1)} %features.3) | copy-start | bytes 147460
  38.0 33.1 %copy-start.1 = (bf16[1,3,64,128]{3,2,1,0:T(8,128)(2,1)S(1)}, bf16[1,3,64,128]{3,2,1,0:T(8,128)(2,1)}, u32[]{:S(2)}) copy-start(bf16[1,3,64,128]{3,2,1,0:T(8,128)(2,1)} %cotangent.3) | copy-start | bytes 147460
  38.0 33.1 %copy-start.2 = (s32[1,3]{1,0:T(1,128)S(1)}, s32[1,3]{1,0:T(1,128)}, u32[]{:S(2)}) copy-start(s32[1,3]{1,0:T(1,128)} %blocks.3) | copy-start | bytes 40
  61.4 21.2 %all-to-all-start.2 = ((bf16[24,14,128]{2,1,0:T(8,128)(2,1)}), bf16[24,14,128]{2,1,0:T(8,128)(2,1)S(1)}, u32[]{:S(2)}, u32[]{:S(2)}) async-start(bf16[24,14,128]{2,1,0:T(8,128)(2,1)} %shard_map.88), calls=%async_computation.2 | async-start | bytes 196608 | tf_op jit(solution)/shard_map/all_to_all | solution.py:450

commit v6 on v5

--- a/solution.py
+++ b/solution.py
@@ -250,16 +250,16 @@
         )
         return jnp.concatenate(parts, axis=0)
 
+    two = fetch([(w_second_hbm.at[k], w_second.at[k]) for k in thirds], sems, 3)
     store_shifted(field_z, field(0), 8)
-    two = fetch([(w_second_hbm.at[k], w_second.at[k]) for k in thirds], sems, 3)
     upstream = field(1)
     store_shifted(upstream_z, upstream, 8)
     pad_store(upstream_pad, upstream)
     for copy in one:
         copy.wait()
-    act_part[...] = spread(taps(field_z, w_first, 8))
     for copy in two:
         copy.wait()
+    act_part[...] = spread(taps(field_z, w_first, 8))
     grad_part[...] = spread(taps(upstream_z, w_second, 8, True))
 
 

time: 83.7 us -> 83.7 us (level)
  transfers between devices with their start and end apart: 4 -> 4, of which waited for: 1 -> 1; matrix products, arithmetic and copies ran while one was open for 0% -> 0% of each run, Pallas kernels for 9% -> 8%
where the time goes in v6:
time: 83.7 us; the launch traced here: 83.2 us
  blocking collectives  36.4 us (43%)
  starting transfers between devices  25.1 us (30%)
  Pallas kernels  12.3 us (15%)
  waiting for transfers between devices  8.5 us (10%)
    all_to_all x1, blocking collectives, on_device(): lax.all_to_all(along_x.transpose(1, 2, 0, 3), 'ya', 0, 0, tiled=True)  23.2 us
    all_to_all x1, blocking collectives, on_device(): lax.all_to_all(terms, ('yb', 'x', 'sb'), 0, 0, tiled=True)  13.1 us
    ppermute x1, starting transfers between devices, on_device(): partner = lax.ppermute(inner, 'c', [(0, 1), (1, 0)])  12.4 us
    all_to_all x1, starting transfers between devices, on_device(): pieces = lax.all_to_all(copies, ('zh', 'c', 'sa', 'sb'), 0, 0, tiled=True)  9.46 us
    all_to_all x1, waiting for transfers between devices, on_device(): pieces = lax.all_to_all(copies, ('zh', 'c', 'sa', 'sb'), 0, 0, tiled=True)  8.49 us
    pallas_call x1, Pallas kernels, on_device(): kernel_call(chip_kernel, [VMEM, VMEM, HBM, HBM], [shape(27, C, C), shape(...  3.81 us
    pallas_call x1, Pallas kernels, on_device(): kernel_call(main_kernel, [VMEM] * 10, [shape(8, 2, 14, 16, C), shape(10,...  3.31 us
    pallas_call x1, Pallas kernels, on_device(): kernel_call(output_kernel, [SMEM] + [VMEM] * 6, [shape(1, SLOTS, 64, C)]...  2.99 us
  transfers between devices with their start and end apart: 4, of which 1 were waited for; matrix products, arithmetic and copies ran while one was open for 0% of the time, Pallas kernels for 8%

profile of v6, /device:TPU:1, one launch (start us, length us, event | category | flops | bytes accessed | tf_op | source)
XLA Modules:
  0.0 83.2 jit_solution(15687939244841437315)
XLA Ops:
  0.6 0.9 %shard_map.84 = (bf16[1,7,32,128]{3,2,1,0:T(8,128)(2,1)S(1)}, bf16[7,64,128]{2,1,0:T(8,128)(2,1)S(1)}) custom-call(s32[1,3]{1,0:T(1,128)} %blocks.3, bf16[1,3,64,128]{3,2,1,0:T(8,128)(2,1)} %features.3, bf16[1,3,64,128]{3,2,1,0:T(8,128)(2,1)} %cotangent.3), custom_call_target="tpu_custom_call" | custom-call | flops 1 | bytes 4000000 | tf_op jit(solution)/shard_map/pallas_call | solution.py:399
  1.6 12.4 %collective-permute-start = (bf16[7,64,128]{2,1,0:T(8,128)(2,1)S(1)}, bf16[7,64,128]{2,1,0:T(8,128)(2,1)S(1)}, u32[]{:S(2)}, u32[]{:S(2)}) collective-permute-start(bf16[7,64,128]{2,1,0:T(8,128)(2,1)S(1)} %get-tuple-element.19.own), channel_id=1, source_target_pairs={{0,6},{6,0},{1,7},{7,1},{2,8},{8,2},{3,9},{9,3},{4,10},{10,4},{5,1... | collective-permute-start | bytes 344072 | tf_op jit(solution)/shard_map/ppermute | solution.py:408
  14.0 1.9 %collective-permute-start.2 = (bf16[1,7,32,128]{3,2,1,0:T(8,128)(2,1)S(1)}, bf16[1,7,32,128]{3,2,1,0:T(8,128)(2,1)S(1)}, u32[]{:S(2)}, u32[]{:S(2)}) collective-permute-start(bf16[1,7,32,128]{3,2,1,0:T(8,128)(2,1)S(1)} %get-tuple-element.20), channel_id=1, source_target_pairs={{6,12},{18,24},{30,36},{42,48},{54,60},{66,72},{78,84},{90,96},{10... | collective-permute-start | bytes 172040 | tf_op jit(solution)/shard_map/ppermute | solution.py:410
  15.9 1.3 %collective-permute-start.1 = (bf16[1,7,32,128]{3,2,1,0:T(8,128)(2,1)S(1)}, bf16[1,7,32,128]{3,2,1,0:T(8,128)(2,1)S(1)}, u32[]{:S(2)}, u32[]{:S(2)}) collective-permute-start(bf16[1,7,32,128]{3,2,1,0:T(8,128)(2,1)S(1)} %get-tuple-element.20), channel_id=1, source_target_pairs={{12,0},{24,12},{36,24},{48,36},{60,48},{72,60},{84,72},{96,84},{10... | collective-permute-start | bytes 172040 | tf_op jit(solution)/shard_map/ppermute | solution.py:409
  17.2 0.0 collective-permute-done.partner
  17.2 3.8 %shard_map.85 = (bf16[27,128,128]{2,1,0:T(8,128)(2,1)S(1)}, bf16[27,128,128]{2,1,0:T(8,128)(2,1)S(1)}, bf16[3,8,10,16,128]{4,3,2,1,0:T(8,128)(2,1)S(1)}, bf16[12...) custom-call(bf16[7,64,128]{2,1,0:T(8,128)(2,1)S(1)} %get-tuple-element.19.own, ...), custom_call_target="tpu_custom_call" | custom-call | flops 2000000000 | bytes 4000000 | tf_op jit(solution)/shard_map/pallas_call | solution.py:411
  21.1 0.0 collective-permute-done.2.near
  21.1 0.0 collective-permute-done.1.far
  21.1 3.3 %shard_map.86 = (bf16[8,2,14,16,128]{4,3,2,1,0:T(8,128)(2,1)S(1)}, bf16[10,8,16,128]{3,2,1,0:T(8,128)(2,1)S(1)}, bf16[10,8,16,128]{3,2,1,0:T(8,128)(2,1)S(1)}) custom-call(bf16[7,64,128]{2,1,0:T(8,128)(2,1)S(1)} %get-tuple-element.19.own, bf16[7,64,128]{2,1,0:T(8,128)(2,1)S(1)} %collective-permute-done.partner, ...), custom_call_target="tpu_custom_call" | custom-call | flops 2000000000 | bytes 4000000 | tf_op jit(solution)/shard_map/pallas_call | solution.py:426
  24.4 13.1 %all_to_all.15 = bf16[16,14,16,128]{3,2,1,0:T(8,128)(2,1)S(1)} all-to-all(bf16[16,14,16,128]{3,2,1,0:T(8,128)(2,1)S(1)} %bitcast.5), channel_id=1, replica_groups=mesh['zh'=2,'ya'=4,'yb'=2,'x'=4,'c'=2,'sa'=3,'sb'=2] {'yb','x','sb'}, dimensions={0} | all-to-all | bytes 1835008 | tf_op jit(solution)/shard_map/all_to_all | solution.py:447
  37.6 0.0 copy-start
  37.6 0.0 copy-start.1
  37.6 0.0 copy-start.2
  37.6 0.1 convert_reduce_fusion
  37.7 23.2 %all_to_all.16 = f32[4,4,14,128]{3,1,2,0:T(4,128)S(1)} all-to-all(f32[4,4,14,128]{3,1,2,0:T(4,128)S(1)} %bitcast.6), channel_id=1, replica_groups=mesh['zh'=2,'ya'=4,'yb'=2,'x'=4,'c'=2,'sa'=3,'sb'=2] {'ya'}, dimensions={0} | all-to-all | bytes 229376 | tf_op jit(solution)/shard_map/all_to_all | solution.py:448
  61.0 0.7 shard_map.88
  61.6 9.5 %all-to-all-start.2 = ((bf16[24,14,128]{2,1,0:T(8,128)(2,1)}), bf16[24,14,128]{2,1,0:T(8,128)(2,1)S(1)}, u32[]{:S(2)}, u32[]{:S(2)}) async-start(bf16[24,14,128]{2,1,0:T(8,128)(2,1)} %shard_map.88), calls=%async_computation.2 | async-start | bytes 196608 | tf_op jit(solution)/shard_map/all_to_all | solution.py:450
  71.1 0.0 copy-done
  71.1 0.0 copy-done.1
  71.1 0.0 copy-done.2
  71.1 3.0 %shard_map.87 = (bf16[1,3,64,128]{3,2,1,0:T(8,128)(2,1)}, bf16[1,3,64,128]{3,2,1,0:T(8,128)(2,1)}) custom-call(s32[1,3]{1,0:T(1,128)S(1)} %copy-done.2, bf16[1,3,64,128]{3,2,1,0:T(8,128)(2,1)S(1)} %copy-done, bf16[1,3,64,128]{3,2,1,0:T(8,128)(2,1)S(1)} %copy-done.1, bf16[10,8,16,128]{3,2,1,0:T(8,128)(2,1)S(1)} %get-tuple-element.27.hidden, ...), custom_call_target="tpu_custom_call" | custom-call | flops 1400000000 | bytes 4000000 | tf_op jit(solution)/shard_map/pallas_call | solution.py:439
  74.1 8.5 %all-to-all-done.2.pieces = bf16[24,14,128]{2,1,0:T(8,128)(2,1)S(1)} async-done(((bf16[24,14,128]{2,1,0:T(8,128)(2,1)}), bf16[24,14,128]{2,1,0:T(8,128)(2,1)S(1)}, u32[]{:S(2)}, u32[]{:S(2)}) %all-to-all-start.2) | async-done | bytes 86048 | tf_op jit(solution)/shard_map/all_to_all | solution.py:450
  82.6 0.6 shard_map.89
  (2 shorter events, 0.0 us)
Async XLA Ops:
  1.6 15.7 %collective-permute-start = (bf16[7,64,128]{2,1,0:T(8,128)(2,1)S(1)}, bf16[7,64,128]{2,1,0:T(8,128)(2,1)S(1)}, u32[]{:S(2)}, u32[]{:S(2)}) collective-permute-start(bf16[7,64,128]{2,1,0:T(8,128)(2,1)S(1)} %get-tuple-element.19.own), channel_id=1, source_target_pairs={{0,6},{6,0},{1,7},{7,1},{2,8},{8,2},{3,9},{9,3},{4,10},{10,4},{5,1... | collective-permute-start | bytes 344072 | tf_op jit(solution)/shard_map/ppermute | solution.py:408
  14.0 7.1 %collective-permute-start.2 = (bf16[1,7,32,128]{3,2,1,0:T(8,128)(2,1)S(1)}, bf16[1,7,32,128]{3,2,1,0:T(8,128)(2,1)S(1)}, u32[]{:S(2)}, u32[]{:S(2)}) collective-permute-start(bf16[1,7,32,128]{3,2,1,0:T(8,128)(2,1)S(1)} %get-tuple-element.20), channel_id=1, source_target_pairs={{6,12},{18,24},{30,36},{42,48},{54,60},{66,72},{78,84},{90,96},{10... | collective-permute-start | bytes 172040 | tf_op jit(solution)/shard_map/ppermute | solution.py:410
  15.9 5.1 %collective-permute-start.1 = (bf16[1,7,32,128]{3,2,1,0:T(8,128)(2,1)S(1)}, bf16[1,7,32,128]{3,2,1,0:T(8,128)(2,1)S(1)}, u32[]{:S(2)}, u32[]{:S(2)}) collective-permute-start(bf16[1,7,32,128]{3,2,1,0:T(8,128)(2,1)S(1)} %get-tuple-element.20), channel_id=1, source_target_pairs={{12,0},{24,12},{36,24},{48,36},{60,48},{72,60},{84,72},{96,84},{10... | collective-permute-start | bytes 172040 | tf_op jit(solution)/shard_map/ppermute | solution.py:409
  37.6 33.5 %copy-start = (bf16[1,3,64,128]{3,2,1,0:T(8,128)(2,1)S(1)}, bf16[1,3,64,128]{3,2,1,0:T(8,128)(2,1)}, u32[]{:S(2)}) copy-start(bf16[1,3,64,128]{3,2,1,0:T(8,128)(2,1)} %features.3) | copy-start | bytes 147460
  37.6 33.6 %copy-start.1 = (bf16[1,3,64,128]{3,2,1,0:T(8,128)(2,1)S(1)}, bf16[1,3,64,128]{3,2,1,0:T(8,128)(2,1)}, u32[]{:S(2)}) copy-start(bf16[1,3,64,128]{3,2,1,0:T(8,128)(2,1)} %cotangent.3) | copy-start | bytes 147460
  37.6 33.6 %copy-start.2 = (s32[1,3]{1,0:T(1,128)S(1)}, s32[1,3]{1,0:T(1,128)}, u32[]{:S(2)}) copy-start(s32[1,3]{1,0:T(1,128)} %blocks.3) | copy-start | bytes 40
  61.6 21.0 %all-to-all-start.2 = ((bf16[24,14,128]{2,1,0:T(8,128)(2,1)}), bf16[24,14,128]{2,1,0:T(8,128)(2,1)S(1)}, u32[]{:S(2)}, u32[]{:S(2)}) async-start(bf16[24,14,128]{2,1,0:T(8,128)(2,1)} %shard_map.88), calls=%async_computation.2 | async-start | bytes 196608 | tf_op jit(solution)/shard_map/all_to_all | solution.py:450

commit v7 on v6

--- a/solution.py
+++ b/solution.py
@@ -286,6 +286,7 @@
     store_shifted(outer_z, field(0), 4)
     store_shifted(outer_up_z, field(1), 4)
     first_act = completed(act_part[...], outer_z, w_first).reshape(10, 8, 16, C)
+    hidden_grad = completed(grad_part[...], outer_up_z, w_second, True).reshape(10, 8, 16, C)
     live = jnp.concatenate(
         [
             live_tiles(left)[None],
@@ -299,7 +300,6 @@
     hidden = live * (first_act * gate)
     hidden_out[...] = hidden.astype(BF16)
     slope = live * (gate * (1.0 + first_act * (1.0 - gate)))
-    hidden_grad = completed(grad_part[...], outer_up_z, w_second, True).reshape(10, 8, 16, C)
     grad_out[...] = (hidden_grad * slope).astype(BF16)
 
     @pl.when(even)

time: 83.7 us -> 83.6 us (level)
  no operation moved by 1% of the time
where the time goes in v7:
time: 83.6 us; the launch traced here: 83.2 us
  blocking collectives  36.4 us (44%)
  starting transfers between devices  25.1 us (30%)
  Pallas kernels  12.3 us (15%)
  waiting for transfers between devices  8.5 us (10%)
    all_to_all x1, blocking collectives, on_device(): lax.all_to_all(along_x.transpose(1, 2, 0, 3), 'ya', 0, 0, tiled=True)  23.2 us
    all_to_all x1, blocking collectives, on_device(): lax.all_to_all(terms, ('yb', 'x', 'sb'), 0, 0, tiled=True)  13.1 us
    ppermute x1, starting transfers between devices, on_device(): partner = lax.ppermute(inner, 'c', [(0, 1), (1, 0)])  12.4 us
    all_to_all x1, starting transfers between devices, on_device(): pieces = lax.all_to_all(copies, ('zh', 'c', 'sa', 'sb'), 0, 0, tiled=True)  9.46 us
    all_to_all x1, waiting for transfers between devices, on_device(): pieces = lax.all_to_all(copies, ('zh', 'c', 'sa', 'sb'), 0, 0, tiled=True)  8.49 us
    pallas_call x1, Pallas kernels, on_device(): kernel_call(chip_kernel, [VMEM, VMEM, HBM, HBM], [shape(27, C, C), shape(...  3.81 us
    pallas_call x1, Pallas kernels, on_device(): kernel_call(main_kernel, [VMEM] * 10, [shape(8, 2, 14, 16, C), shape(10,...  3.3 us
    pallas_call x1, Pallas kernels, on_device(): kernel_call(output_kernel, [SMEM] + [VMEM] * 6, [shape(1, SLOTS, 64, C)]...  2.99 us
  transfers between devices with their start and end apart: 4, of which 1 were waited for; matrix products, arithmetic and copies ran while one was open for 0% of the time, Pallas kernels for 8%

profile of v7, /device:TPU:1, one launch (start us, length us, event | category | flops | bytes accessed | tf_op | source)
XLA Modules:
  0.0 83.2 jit_solution(15264522121065281813)
XLA Ops:
  0.6 0.9 %shard_map.84 = (bf16[1,7,32,128]{3,2,1,0:T(8,128)(2,1)S(1)}, bf16[7,64,128]{2,1,0:T(8,128)(2,1)S(1)}) custom-call(s32[1,3]{1,0:T(1,128)} %blocks.3, bf16[1,3,64,128]{3,2,1,0:T(8,128)(2,1)} %features.3, bf16[1,3,64,128]{3,2,1,0:T(8,128)(2,1)} %cotangent.3), custom_call_target="tpu_custom_call" | custom-call | flops 1 | bytes 4000000 | tf_op jit(solution)/shard_map/pallas_call | solution.py:399
  1.6 12.4 %collective-permute-start = (bf16[7,64,128]{2,1,0:T(8,128)(2,1)S(1)}, bf16[7,64,128]{2,1,0:T(8,128)(2,1)S(1)}, u32[]{:S(2)}, u32[]{:S(2)}) collective-permute-start(bf16[7,64,128]{2,1,0:T(8,128)(2,1)S(1)} %get-tuple-element.19.own), channel_id=1, source_target_pairs={{0,6},{6,0},{1,7},{7,1},{2,8},{8,2},{3,9},{9,3},{4,10},{10,4},{5,1... | collective-permute-start | bytes 344072 | tf_op jit(solution)/shard_map/ppermute | solution.py:408
  14.0 1.9 %collective-permute-start.2 = (bf16[1,7,32,128]{3,2,1,0:T(8,128)(2,1)S(1)}, bf16[1,7,32,128]{3,2,1,0:T(8,128)(2,1)S(1)}, u32[]{:S(2)}, u32[]{:S(2)}) collective-permute-start(bf16[1,7,32,128]{3,2,1,0:T(8,128)(2,1)S(1)} %get-tuple-element.20), channel_id=1, source_target_pairs={{6,12},{18,24},{30,36},{42,48},{54,60},{66,72},{78,84},{90,96},{10... | collective-permute-start | bytes 172040 | tf_op jit(solution)/shard_map/ppermute | solution.py:410
  15.9 1.3 %collective-permute-start.1 = (bf16[1,7,32,128]{3,2,1,0:T(8,128)(2,1)S(1)}, bf16[1,7,32,128]{3,2,1,0:T(8,128)(2,1)S(1)}, u32[]{:S(2)}, u32[]{:S(2)}) collective-permute-start(bf16[1,7,32,128]{3,2,1,0:T(8,128)(2,1)S(1)} %get-tuple-element.20), channel_id=1, source_target_pairs={{12,0},{24,12},{36,24},{48,36},{60,48},{72,60},{84,72},{96,84},{10... | collective-permute-start | bytes 172040 | tf_op jit(solution)/shard_map/ppermute | solution.py:409
  17.2 0.0 collective-permute-done.partner
  17.2 3.8 %shard_map.85 = (bf16[27,128,128]{2,1,0:T(8,128)(2,1)S(1)}, bf16[27,128,128]{2,1,0:T(8,128)(2,1)S(1)}, bf16[3,8,10,16,128]{4,3,2,1,0:T(8,128)(2,1)S(1)}, bf16[12...) custom-call(bf16[7,64,128]{2,1,0:T(8,128)(2,1)S(1)} %get-tuple-element.19.own, ...), custom_call_target="tpu_custom_call" | custom-call | flops 2000000000 | bytes 4000000 | tf_op jit(solution)/shard_map/pallas_call | solution.py:411
  21.1 0.0 collective-permute-done.2.near
  21.1 0.0 collective-permute-done.1.far
  21.1 3.3 %shard_map.86 = (bf16[8,2,14,16,128]{4,3,2,1,0:T(8,128)(2,1)S(1)}, bf16[10,8,16,128]{3,2,1,0:T(8,128)(2,1)S(1)}, bf16[10,8,16,128]{3,2,1,0:T(8,128)(2,1)S(1)}) custom-call(bf16[7,64,128]{2,1,0:T(8,128)(2,1)S(1)} %get-tuple-element.19.own, bf16[7,64,128]{2,1,0:T(8,128)(2,1)S(1)} %collective-permute-done.partner, ...), custom_call_target="tpu_custom_call" | custom-call | flops 2000000000 | bytes 4000000 | tf_op jit(solution)/shard_map/pallas_call | solution.py:426
  24.4 13.1 %all_to_all.15 = bf16[16,14,16,128]{3,2,1,0:T(8,128)(2,1)S(1)} all-to-all(bf16[16,14,16,128]{3,2,1,0:T(8,128)(2,1)S(1)} %bitcast.5), channel_id=1, replica_groups=mesh['zh'=2,'ya'=4,'yb'=2,'x'=4,'c'=2,'sa'=3,'sb'=2] {'yb','x','sb'}, dimensions={0} | all-to-all | bytes 1835008 | tf_op jit(solution)/shard_map/all_to_all | solution.py:447
  37.5 0.0 copy-start
  37.5 0.0 copy-start.1
  37.5 0.0 copy-start.2
  37.5 0.1 convert_reduce_fusion
  37.7 23.2 %all_to_all.16 = f32[4,4,14,128]{3,1,2,0:T(4,128)S(1)} all-to-all(f32[4,4,14,128]{3,1,2,0:T(4,128)S(1)} %bitcast.6), channel_id=1, replica_groups=mesh['zh'=2,'ya'=4,'yb'=2,'x'=4,'c'=2,'sa'=3,'sb'=2] {'ya'}, dimensions={0} | all-to-all | bytes 229376 | tf_op jit(solution)/shard_map/all_to_all | solution.py:448
  61.0 0.7 shard_map.88
  61.6 9.5 %all-to-all-start.2 = ((bf16[24,14,128]{2,1,0:T(8,128)(2,1)}), bf16[24,14,128]{2,1,0:T(8,128)(2,1)S(1)}, u32[]{:S(2)}, u32[]{:S(2)}) async-start(bf16[24,14,128]{2,1,0:T(8,128)(2,1)} %shard_map.88), calls=%async_computation.2 | async-start | bytes 196608 | tf_op jit(solution)/shard_map/all_to_all | solution.py:450
  71.1 0.0 copy-done
  71.1 0.0 copy-done.1
  71.1 0.0 copy-done.2
  71.1 3.0 %shard_map.87 = (bf16[1,3,64,128]{3,2,1,0:T(8,128)(2,1)}, bf16[1,3,64,128]{3,2,1,0:T(8,128)(2,1)}) custom-call(s32[1,3]{1,0:T(1,128)S(1)} %copy-done.2, bf16[1,3,64,128]{3,2,1,0:T(8,128)(2,1)S(1)} %copy-done, bf16[1,3,64,128]{3,2,1,0:T(8,128)(2,1)S(1)} %copy-done.1, bf16[10,8,16,128]{3,2,1,0:T(8,128)(2,1)S(1)} %get-tuple-element.27.hidden, ...), custom_call_target="tpu_custom_call" | custom-call | flops 1400000000 | bytes 4000000 | tf_op jit(solution)/shard_map/pallas_call | solution.py:439
  74.1 8.5 %all-to-all-done.2.pieces = bf16[24,14,128]{2,1,0:T(8,128)(2,1)S(1)} async-done(((bf16[24,14,128]{2,1,0:T(8,128)(2,1)}), bf16[24,14,128]{2,1,0:T(8,128)(2,1)S(1)}, u32[]{:S(2)}, u32[]{:S(2)}) %all-to-all-start.2) | async-done | bytes 86048 | tf_op jit(solution)/shard_map/all_to_all | solution.py:450
  82.6 0.6 shard_map.89
  (2 shorter events, 0.0 us)
Async XLA Ops:
  1.6 15.7 %collective-permute-start = (bf16[7,64,128]{2,1,0:T(8,128)(2,1)S(1)}, bf16[7,64,128]{2,1,0:T(8,128)(2,1)S(1)}, u32[]{:S(2)}, u32[]{:S(2)}) collective-permute-start(bf16[7,64,128]{2,1,0:T(8,128)(2,1)S(1)} %get-tuple-element.19.own), channel_id=1, source_target_pairs={{0,6},{6,0},{1,7},{7,1},{2,8},{8,2},{3,9},{9,3},{4,10},{10,4},{5,1... | collective-permute-start | bytes 344072 | tf_op jit(solution)/shard_map/ppermute | solution.py:408
  14.0 7.1 %collective-permute-start.2 = (bf16[1,7,32,128]{3,2,1,0:T(8,128)(2,1)S(1)}, bf16[1,7,32,128]{3,2,1,0:T(8,128)(2,1)S(1)}, u32[]{:S(2)}, u32[]{:S(2)}) collective-permute-start(bf16[1,7,32,128]{3,2,1,0:T(8,128)(2,1)S(1)} %get-tuple-element.20), channel_id=1, source_target_pairs={{6,12},{18,24},{30,36},{42,48},{54,60},{66,72},{78,84},{90,96},{10... | collective-permute-start | bytes 172040 | tf_op jit(solution)/shard_map/ppermute | solution.py:410
  15.9 5.1 %collective-permute-start.1 = (bf16[1,7,32,128]{3,2,1,0:T(8,128)(2,1)S(1)}, bf16[1,7,32,128]{3,2,1,0:T(8,128)(2,1)S(1)}, u32[]{:S(2)}, u32[]{:S(2)}) collective-permute-start(bf16[1,7,32,128]{3,2,1,0:T(8,128)(2,1)S(1)} %get-tuple-element.20), channel_id=1, source_target_pairs={{12,0},{24,12},{36,24},{48,36},{60,48},{72,60},{84,72},{96,84},{10... | collective-permute-start | bytes 172040 | tf_op jit(solution)/shard_map/ppermute | solution.py:409
  37.5 33.5 %copy-start = (bf16[1,3,64,128]{3,2,1,0:T(8,128)(2,1)S(1)}, bf16[1,3,64,128]{3,2,1,0:T(8,128)(2,1)}, u32[]{:S(2)}) copy-start(bf16[1,3,64,128]{3,2,1,0:T(8,128)(2,1)} %features.3) | copy-start | bytes 147460
  37.5 33.6 %copy-start.1 = (bf16[1,3,64,128]{3,2,1,0:T(8,128)(2,1)S(1)}, bf16[1,3,64,128]{3,2,1,0:T(8,128)(2,1)}, u32[]{:S(2)}) copy-start(bf16[1,3,64,128]{3,2,1,0:T(8,128)(2,1)} %cotangent.3) | copy-start | bytes 147460
  37.5 33.6 %copy-start.2 = (s32[1,3]{1,0:T(1,128)S(1)}, s32[1,3]{1,0:T(1,128)}, u32[]{:S(2)}) copy-start(s32[1,3]{1,0:T(1,128)} %blocks.3) | copy-start | bytes 40
  61.6 21.0 %all-to-all-start.2 = ((bf16[24,14,128]{2,1,0:T(8,128)(2,1)}), bf16[24,14,128]{2,1,0:T(8,128)(2,1)S(1)}, u32[]{:S(2)}, u32[]{:S(2)}) async-start(bf16[24,14,128]{2,1,0:T(8,128)(2,1)} %shard_map.88), calls=%async_computation.2 | async-start | bytes 196608 | tf_op jit(solution)/shard_map/all_to_all | solution.py:450
